TPU v7x, 128 devices: a whole 4x4x4 slice. The times are simulated.
128 devices in a mesh: leaf: 32 (over x, z, y_lo), grid: 4 (over y_hi, core).
Axes of the slice: x: 4, y: 4 (y_hi: 2, y_lo: 2; y = y_hi * 2 + y_lo), z: 4, core: 2. Of those that a mesh axis runs over, the one named last changes fastest.
Arguments:
- rhs_rows: float32 [65536, 256], P(('leaf', 'grid')), may hold values from -6 to 6
- order: int32 [65536], P(('leaf', 'grid')), may hold values from 0 to 511, as said below
- leaf_inverse: float32 [65536, 2048], P('leaf', 'grid'), as said below
- leaf_panels: float32 [32, 6, 1024, 2048], P('leaf', None, None, 'grid'), may hold values from -0.0234375 to 0.0234375
- panel_mask: int32 [32, 6, 16], P('leaf', None, 'grid'), may hold values 0 or 1
- sep_rhs: float32 [32, 1024, 256], P('leaf', None, 'grid'), may hold values from -6 to 6
- sep_inverse: float32 [32, 1024, 1024], P('leaf'), as said below
- sep_panels: float32 [32, 5, 1024, 1024], P('leaf'), may hold values from -0.03125 to 0.03125
Outputs:
- leaf_solution: float32 [65536, 256], P(('leaf', 'grid'))
- sep_solution: float32 [32, 1024, 256], P('leaf', None, 'grid')
- widths: float32 [256], P('grid')
Inputs may be any that keep to these rules, and one draw needn't show every extreme that they name: Each row block of 512 entries of order is a permutation of 0 .. 511. Each leaf's block of leaf_inverse is lower triangular. Each separator's block of sep_inverse is lower triangular.
All inputs are finite; a program needn't handle non-finite values. No bound on the sum of `panel_mask` on one device may be relied on, other than what follows from the above.
Results may differ from a plain program's by a relative error of at most 0.0001.
Values sent between devices are 32-bit elements; how exact they have to be, the bound alone decides.
A program may use at most 192 MiB of HBM per device.

v0:
```python
import jax
import jax.numpy as jnp
from jax import lax
from jax.sharding import PartitionSpec as P


def passed_along(value, axis, steps):
    count = lax.axis_size(axis)
    initial, last = (max(0, -steps), min(count, count - steps))
    return lax.ppermute(value, axis, [(source, source + steps) for source in range(initial, last)])


def local(rhs_rows, order, leaf_inverse, leaf_panels, panel_mask, sep_rhs, sep_inverse, sep_panels):
    highest = lax.Precision.HIGHEST
    n_leaf = lax.axis_size("leaf")
    n_grid = lax.axis_size("grid")
    tiers = leaf_panels.shape[1]
    block_rows = rhs_rows.shape[0]
    columns = rhs_rows.shape[1]
    block_count = n_leaf * n_grid
    slots = block_rows // block_count
    picked = jnp.take(rhs_rows, order, axis=0)
    moved = lax.all_to_all(
        picked.reshape(block_count, slots, columns),
        ("leaf", "grid"),
        split_axis=0,
        concat_axis=0,
        tiled=True,
    )
    local_rhs = moved.reshape(block_rows, columns)
    leaf_y = lax.psum_scatter(
        jnp.dot(leaf_inverse, local_rhs, precision=highest, preferred_element_type=jnp.float32),
        "grid",
        scatter_dimension=0,
        tiled=True,
    )
    column_mask = jnp.repeat(panel_mask[0].astype(jnp.float32), 128, axis=1)
    masked = leaf_panels[0] * column_mask[:, None, :]
    partial_update = jnp.einsum("tsr,rk->tsk", masked, leaf_y, precision=highest)
    pending = lax.psum_scatter(partial_update, "grid", scatter_dimension=2, tiled=True)
    leaf_index = lax.axis_index("leaf")
    level = jnp.ones((), jnp.int32)
    for bit in range(1, tiers):
        level = level + ((leaf_index + 1) % 2**bit == 0).astype(jnp.int32)
    own_rhs = sep_rhs[0]
    own_inverse = sep_inverse[0]
    own_panels = sep_panels[0]
    solved = jnp.zeros_like(own_rhs)
    tail = pending
    for tier in range(1, tiers + 1):
        reach = 1 if tier == 1 else 2 ** (tier - 2)
        right = passed_along(tail, "leaf", -reach)
        if tier == 1:
            left = tail
        else:
            left = passed_along(tail, "leaf", reach)
        is_host = level == tier
        tail = jnp.where(is_host, left + right, tail)

        def solve(operands, tier=tier):
            tail_in, solved_in = operands
            rhs = own_rhs - tail_in[0]
            result = jnp.dot(
                own_inverse, rhs, precision=highest, preferred_element_type=jnp.float32
            )
            rows_new = [tail_in[0]]
            for step in range(tiers - tier):
                rows_new.append(
                    tail_in[1 + step]
                    + jnp.dot(
                        own_panels[step],
                        result,
                        precision=highest,
                        preferred_element_type=jnp.float32,
                    )
                )
            return (jnp.stack(rows_new), result)

        def keep(operands):
            return operands

        tail, solved = lax.cond(is_host, solve, keep, (tail, solved))
        tail = tail[1:]
    grid_index = lax.axis_index("grid")
    own_width = solved.shape[1]
    leaf_squares = jnp.sum(leaf_y * leaf_y, axis=0)
    sep_squares = jnp.sum(solved * solved, axis=0)
    placed = lax.dynamic_update_slice(
        jnp.zeros((columns,), jnp.float32), sep_squares, (grid_index * own_width,)
    )
    total = lax.psum(leaf_squares + placed, ("leaf", "grid"))
    count = n_leaf * (block_rows * n_grid + solved.shape[0])
    widths = jnp.sqrt(total / count + 1e-06)
    mine = lax.dynamic_slice_in_dim(widths, grid_index * own_width, own_width)
    return (leaf_y, solved[None], mine)


def solution(mesh):
    placed = (
        P(("leaf", "grid"), None),
        P(("leaf", "grid")),
        P("leaf", "grid"),
        P("leaf", None, None, "grid"),
        P("leaf", None, "grid"),
        P("leaf", None, "grid"),
        P("leaf", None, None),
        P("leaf", None, None, None),
    )
    return jax.shard_map(
        local,
        mesh=mesh,
        in_specs=placed,
        out_specs=(P(("leaf", "grid"), None), P("leaf", None, "grid"), P("grid")),
        check_vma=False,
    )
```

profile of v0, /device:TPU:16, one launch (start us, length us, event | category | flops | bytes accessed | tf_op | source)
XLA Modules:
  0.0 585.0 jit_solution(16382576553288189884)
XLA Ops:
  10.7 22.2 %all_to_all.5 = f32[128,4,256]{2,1,0:T(4,128)S(1)} all-to-all(f32[128,4,256]{2,1,0:T(4,128)S(1)} %broadcast_select_fusion), channel_id=1, replica_groups=mesh['leaf'=32,'grid'=4] {'leaf','grid'}, dimensions={0} | all-to-all | bytes 1048576 | tf_op jit(solution)/shard_map/all_to_all | solution.py:23
  33.2 10.3 %convolution_bitcast_fusion.1 = f32[2048,256]{0,1:T(8,128)} fusion(f32[512,256]{1,0:T(8,128)S(1)} %reshape.23, f32[2048,512]{1,0:T(8,128)} %param.22), kind=kOutput, calls=%fused_computation.123 | convolution fusion | flops 3221225472 | bytes 6815744 | tf_op jit(solution)/shard_map/dot_general | solution.py:32
  43.9 33.0 %reduce-scatter.3.cloned.1.call-done = f32[512,256]{0,1:T(8,128)} async-done(((f32[2048,256]{0,1:T(8,128)}), f32[512,256]{0,1:T(8,128)}) %reduce-scatter.3.cloned.1.call-update) | async-done | bytes 524304 | tf_op jit(solution)/shard_map/reduce_scatter | solution.py:31
  76.8 16.4 %fusion.208 = f32[6,1024,256]{1,2,0:T(8,128)} fusion(f32[1,6,1024,512]{3,2,1,0:T(8,128)} %param.23, f32[6,512]{1,0:T(8,128)S(1)} %bitcast.399, f32[512,256]{0,1:T(8,128)} %reduce-scatter.3.cloned.1.call-done), kind=kOutput, calls=%fused_computation.121 | convolution fusion | flops 9666822144 | bytes 19410944 | tf_op jit(solution)/shard_map/tsr,rk->tsk/dot_general | solution.py:39
  93.2 64.9 %reduce-scatter.5.cloned.1.call-done = f32[6,1024,64]{1,2,0:T(8,128)} async-done(((f32[6,1024,256]{1,2,0:T(8,128)}), f32[6,1024,64]{1,2,0:T(8,128)}) %reduce-scatter.5.cloned.1.call-update) | async-done | bytes 1572880 | tf_op jit(solution)/shard_map/reduce_scatter | solution.py:40
  159.6 37.4 %collective-permute-done = f32[6,1024,64]{1,2,0:T(8,128)} collective-permute-done((f32[6,1024,64]{1,2,0:T(8,128)}, f32[6,1024,64]{1,2,0:T(8,128)}, u32[]{:S(2)}, u32[]{:S(2)}) %collective-permute-start) | collective-permute-done | bytes 1572896 | tf_op jit(solution)/shard_map/ppermute | solution.py:10
  197.0 2.2 add_select_fusion
  199.2 39.9 %conditional.6 = (f32[6,1024,64]{1,2,0:T(8,128)S(1)}, f32[1024,64]{0,1:T(8,128)}) conditional(s32[]{:T(128)} %convert_element_type.49, f32[6,1024,64]{1,2,0:T(8,128)S(1)} %add_select_fusion, (f32[6,1024,64]{1,2,0:T(8,128)S(1)}, f32[1024,64]{1,0:T(8,128)S(1)}, f32[1024,1024]{1,0:T(8,128)}, f32[5,1024,1024]{2,1,0:T(8,128)}) %tuple.132), branch_computations={%region_2.3_spmd, %region_3.4_spmd} | conditional | flops 4832231424 | bytes 34078736 | solution.py:82
  199.6 7.0 %fusion.75 = f32[64,1024]{1,0:T(8,128)} fusion(f32[1024,1024]{1,0:T(8,128)} %get-tuple-element.103, f32[1024,64]{0,1:T(8,128)S(1)} %copy.24, f32[6,1024,64]{1,2,0:T(8,128)S(1)} %get-tuple-element.101), kind=kOutput, calls=%fused_computation.37 | convolution fusion | flops 805371904 | bytes 4980736 | tf_op jit(solution)/shard_map/cond/branch_1_fun/dot_general | solution.py:63
  206.6 6.4 %fusion.24 = f32[6,1024,64]{1,2,0:T(8,128)S(1)} fusion(f32[6,1024,64]{1,2,0:T(8,128)S(1)} %slice_dynamic-update-slice_fusion, f32[64,1024]{1,0:T(8,128)} %fusion.75, f32[5,1024,1024]{2,1,0:T(8,128)} %get-tuple-element.104, f32[6,1024,64]{1,2,0:T(8,128)S(1)} %get-tuple-element.101), kind=kOutput, calls=%fused_computation.19 | convolution fusion | flops 805371904 | bytes 4980736 | tf_op jit(solution)/shard_map/cond/branch_1_fun/dot_general | solution.py:70
  212.9 6.4 %fusion.36 = f32[6,1024,64]{1,2,0:T(8,128)S(1)} fusion(f32[6,1024,64]{1,2,0:T(8,128)S(1)} %fusion.24, f32[64,1024]{1,0:T(8,128)} %fusion.75, f32[5,1024,1024]{2,1,0:T(8,128)} %get-tuple-element.104, f32[6,1024,64]{1,2,0:T(8,128)S(1)} %get-tuple-element.101), kind=kOutput, calls=%fused_computation.23 | convolution fusion | flops 805371904 | bytes 4980736 | tf_op jit(solution)/shard_map/cond/branch_1_fun/dot_general | solution.py:70
  219.3 6.7 %fusion.48 = f32[6,1024,64]{1,2,0:T(8,128)S(1)} fusion(f32[6,1024,64]{1,2,0:T(8,128)S(1)} %fusion.36, f32[64,1024]{1,0:T(8,128)} %fusion.75, f32[5,1024,1024]{2,1,0:T(8,128)} %get-tuple-element.104, f32[6,1024,64]{1,2,0:T(8,128)S(1)} %get-tuple-element.101), kind=kOutput, calls=%fused_computation.27 | convolution fusion | flops 805371904 | bytes 4980736 | tf_op jit(solution)/shard_map/cond/branch_1_fun/dot_general | solution.py:70
  226.0 6.4 %fusion.60 = f32[6,1024,64]{1,2,0:T(8,128)S(1)} fusion(f32[6,1024,64]{1,2,0:T(8,128)S(1)} %fusion.48, f32[64,1024]{1,0:T(8,128)} %fusion.75, f32[5,1024,1024]{2,1,0:T(8,128)} %get-tuple-element.104, f32[6,1024,64]{1,2,0:T(8,128)S(1)} %get-tuple-element.101), kind=kOutput, calls=%fused_computation.31 | convolution fusion | flops 805371904 | bytes 4980736 | tf_op jit(solution)/shard_map/cond/branch_1_fun/dot_general | solution.py:70
  232.4 6.4 %fusion.72 = f32[6,1024,64]{1,2,0:T(8,128)S(1)} fusion(f32[6,1024,64]{1,2,0:T(8,128)S(1)} %fusion.60, f32[64,1024]{1,0:T(8,128)} %fusion.75, f32[5,1024,1024]{2,1,0:T(8,128)} %get-tuple-element.104, f32[6,1024,64]{1,2,0:T(8,128)S(1)} %get-tuple-element.101), kind=kOutput, calls=%fused_computation.35 | convolution fusion | flops 805371904 | bytes 4980736 | tf_op jit(solution)/shard_map/cond/branch_1_fun/dot_general | solution.py:70
  240.3 2.4 collective-permute-start.1
  243.9 53.8 %collective-permute-done.1 = f32[5,1024,64]{1,2,0:T(8,128)} collective-permute-done((f32[5,1024,64]{1,2,0:T(8,128)}, f32[5,1024,64]{1,2,0:T(8,128)}, u32[]{:S(2)}, u32[]{:S(2)}) %collective-permute-start.1) | collective-permute-done | bytes 1310752 | tf_op jit(solution)/shard_map/ppermute | solution.py:10
  297.7 3.8 collective-permute-done.2
  301.5 3.2 add_select_fusion.1
  304.7 10.7 %conditional.7 = (f32[1024,64]{0,1:T(8,128)}, f32[4,1024,64]{1,2,0:T(8,128)S(1)}) conditional(s32[]{:T(128)} %convert_element_type.48, (f32[5,1024,64]{1,2,0:T(8,128)}, f32[1024,64]{0,1:T(8,128)}) %tuple.75, (f32[5,1024,64]{1,2,0:T(8,128)}, f32[1024,64]{1,0:T(8,128)S(1)}, f32[1024,1024]{1,0:T(8,128)}, f32[5,1024,1024]{2,1,0:T(8,128)}) %tuple.133), branch_computations={%region_4.5_spmd, %region_5.6_spmd} | conditional | flops 4027645952 | bytes 27525136 | solution.py:82
  315.4 3.5 collective-permute-start.3
  320.2 19.6 %collective-permute-done.3 = f32[4,1024,64]{1,2,0:T(8,128)S(1)} collective-permute-done((f32[4,1024,64]{1,2,0:T(8,128)S(1)}, f32[4,1024,64]{1,2,0:T(8,128)S(1)}, u32[]{:S(2)}, u32[]{:S(2)}) %collective-permute-start.3) | collective-permute-done | bytes 1048608 | tf_op jit(solution)/shard_map/ppermute | solution.py:10
  340.8 3.3 collective-permute-done.4
  344.1 1.8 add_select_fusion.2
  346.2 4.2 collective-permute-start.5
  351.6 29.9 %collective-permute-done.5 = f32[3,1024,64]{1,2,0:T(8,128)S(1)} collective-permute-done((f32[3,1024,64]{1,2,0:T(8,128)S(1)}, f32[3,1024,64]{1,2,0:T(8,128)S(1)}, u32[]{:S(2)}, u32[]{:S(2)}) %collective-permute-start.5) | collective-permute-done | bytes 786464 | tf_op jit(solution)/shard_map/ppermute | solution.py:10
  382.9 8.0 %collective-permute-start.7 = (f32[2,1024,64]{1,2,0:T(8,128)S(1)}, f32[2,1024,64]{1,2,0:T(8,128)S(1)}, u32[]{:S(2)}, u32[]{:S(2)}) collective-permute-start(f32[2,1024,64]{1,2,0:T(8,128)S(1)} %get-tuple-element.156), channel_id=1, source_target_pairs={{0,32},{4,36},{8,40},{12,44},{16,48},{20,52},{24,56},{28,60},{32,6... | collective-permute-start | bytes 1572872 | tf_op jit(solution)/shard_map/ppermute | solution.py:10
  392.2 7.9 %collective-permute-done.7 = f32[2,1024,64]{1,2,0:T(8,128)S(1)} collective-permute-done((f32[2,1024,64]{1,2,0:T(8,128)S(1)}, f32[2,1024,64]{1,2,0:T(8,128)S(1)}, u32[]{:S(2)}, u32[]{:S(2)}) %collective-permute-start.7) | collective-permute-done | bytes 524320 | tf_op jit(solution)/shard_map/ppermute | solution.py:10
  400.2 7.3 %collective-permute-done.8 = f32[2,1024,64]{1,2,0:T(8,128)S(1)} collective-permute-done((f32[2,1024,64]{1,2,0:T(8,128)S(1)}, f32[2,1024,64]{1,2,0:T(8,128)S(1)}, u32[]{:S(2)}, u32[]{:S(2)}) %collective-permute-start.8) | collective-permute-done | bytes 524320 | tf_op jit(solution)/shard_map/ppermute | solution.py:10
  407.5 2.1 conditional.10
  410.9 6.1 %collective-permute-start.9 = (f32[1,1024,64]{2,1,0:T(8,128)S(1)}, f32[1,1024,64]{2,1,0:T(8,128)S(1)}, u32[]{:S(2)}, u32[]{:S(2)}) collective-permute-start(f32[1,1024,64]{2,1,0:T(8,128)S(1)} %get-tuple-element.221), channel_id=1, source_target_pairs={{0,64},{4,68},{8,72},{12,76},{16,80},{20,84},{24,88},{28,92},{32,9... | collective-permute-start | bytes 786440 | tf_op jit(solution)/shard_map/ppermute | solution.py:10
  418.2 7.8 %collective-permute-done.10 = f32[1,1024,64]{2,1,0:T(8,128)S(1)} collective-permute-done((f32[1,1024,64]{2,1,0:T(8,128)S(1)}, f32[1,1024,64]{2,1,0:T(8,128)S(1)}, u32[]{:S(2)}, u32[]{:S(2)}) %collective-permute-start.10) | collective-permute-done | bytes 262176 | tf_op jit(solution)/shard_map/ppermute | solution.py:10
  428.5 148.9 %psum.7 = f32[256]{0:T(256)S(1)} all-reduce(f32[256]{0:T(256)S(1)} %add_dynamic-update-slice_fusion), channel_id=1, replica_groups=mesh['leaf'=32,'grid'=4] {'leaf','grid'}, use_global_device_ids=true, to_apply=%region_17.18 | all-reduce | flops 256 | bytes 2048 | tf_op jit(solution)/shard_map/psum | solution.py:91
  (59 shorter events, 23.8 us)
Async XLA Ops:
  7.2 1.5 copy-start
  7.2 69.7 %reduce-scatter.3.cloned.1.call-start = ((), (), s32[]{:S(2)}) async-start(), calls=%async_computation.3 | async-start | bytes 2621440 | tf_op jit(solution)/shard_map/reduce_scatter | solution.py:31
  33.1 10.6 %copy-start.6 = (s32[1,6,4]{1,2,0:T(4,128)S(1)}, s32[1,6,4]{1,2,0:T(4,128)}, u32[]{:S(2)}) copy-start(s32[1,6,4]{1,2,0:T(4,128)} %param.24) | copy-start | bytes 292
  43.5 114.6 %reduce-scatter.5.cloned.1.call-start = ((), (), s32[]{:S(2)}) async-start(), calls=%async_computation.4 | async-start | bytes 7864320 | tf_op jit(solution)/shard_map/reduce_scatter | solution.py:40
  93.2 66.2 %copy-start.5 = (f32[1,1024,64]{1,2,0:T(8,128)S(1)}, f32[1,1024,64]{1,2,0:T(8,128)}, u32[]{:S(2)}) copy-start(f32[1,1024,64]{1,2,0:T(8,128)} %param.25) | copy-start | bytes 786436
  158.1 38.9 %collective-permute-start = (f32[6,1024,64]{1,2,0:T(8,128)}, f32[6,1024,64]{1,2,0:T(8,128)}, u32[]{:S(2)}, u32[]{:S(2)}) collective-permute-start(f32[6,1024,64]{1,2,0:T(8,128)} %reduce-scatter.5.cloned.1.call-done), channel_id=1, source_target_pairs={{4,0},{8,4},{12,8},{16,12},{20,16},{24,20},{28,24},{32,28},{36,32}... | collective-permute-start | bytes 4718600 | tf_op jit(solution)/shard_map/ppermute | solution.py:10
  240.3 57.4 %collective-permute-start.1 = (f32[5,1024,64]{1,2,0:T(8,128)}, f32[5,1024,64]{1,2,0:T(8,128)}, u32[]{:S(2)}, u32[]{:S(2)}) collective-permute-start(f32[5,1024,64]{1,2,0:T(8,128)} %slice.136), channel_id=1, source_target_pairs={{0,4},{4,8},{8,12},{12,16},{16,20},{20,24},{24,28},{28,32},{32,36}... | collective-permute-start | bytes 3932168 | tf_op jit(solution)/shard_map/ppermute | solution.py:10
  242.6 58.9 %collective-permute-start.2 = (f32[5,1024,64]{1,2,0:T(8,128)}, f32[5,1024,64]{1,2,0:T(8,128)}, u32[]{:S(2)}, u32[]{:S(2)}) collective-permute-start(f32[5,1024,64]{1,2,0:T(8,128)} %slice.136), channel_id=1, source_target_pairs={{4,0},{8,4},{12,8},{16,12},{20,16},{24,20},{28,24},{32,28},{36,32}... | collective-permute-start | bytes 3932168 | tf_op jit(solution)/shard_map/ppermute | solution.py:10
  315.4 24.4 %collective-permute-start.3 = (f32[4,1024,64]{1,2,0:T(8,128)S(1)}, f32[4,1024,64]{1,2,0:T(8,128)S(1)}, u32[]{:S(2)}, u32[]{:S(2)}) collective-permute-start(f32[4,1024,64]{1,2,0:T(8,128)S(1)} %get-tuple-element.152), channel_id=1, source_target_pairs={{0,8},{4,12},{8,16},{12,20},{16,24},{20,28},{24,32},{28,36},{32,40... | collective-permute-start | bytes 3145736 | tf_op jit(solution)/shard_map/ppermute | solution.py:10
  318.9 25.1 %collective-permute-start.4 = (f32[4,1024,64]{1,2,0:T(8,128)S(1)}, f32[4,1024,64]{1,2,0:T(8,128)}, u32[]{:S(2)}, u32[]{:S(2)}) collective-permute-start(f32[4,1024,64]{1,2,0:T(8,128)S(1)} %get-tuple-element.152), channel_id=1, source_target_pairs={{8,0},{12,4},{16,8},{20,12},{24,16},{28,20},{32,24},{36,28},{40,32... | collective-permute-start | bytes 3145736 | tf_op jit(solution)/shard_map/ppermute | solution.py:10
  339.8 1.0 copy-start.4
  346.2 35.3 %copy-start.3 = (f32[3,1024,64]{1,2,0:T(8,128)}, f32[3,1024,64]{1,2,0:T(8,128)S(1)}, u32[]{:S(2)}) copy-start(f32[3,1024,64]{1,2,0:T(8,128)S(1)} %get-tuple-element.154) | copy-start | bytes 2359300
  346.2 35.3 %collective-permute-start.5 = (f32[3,1024,64]{1,2,0:T(8,128)S(1)}, f32[3,1024,64]{1,2,0:T(8,128)S(1)}, u32[]{:S(2)}, u32[]{:S(2)}) collective-permute-start(f32[3,1024,64]{1,2,0:T(8,128)S(1)} %get-tuple-element.154), channel_id=1, source_target_pairs={{0,16},{4,20},{8,24},{12,28},{16,32},{20,36},{24,40},{28,44},{32,4... | collective-permute-start | bytes 2359304 | tf_op jit(solution)/shard_map/ppermute | solution.py:10
  350.3 31.2 %collective-permute-start.6 = (f32[3,1024,64]{1,2,0:T(8,128)S(1)}, f32[3,1024,64]{1,2,0:T(8,128)S(1)}, u32[]{:S(2)}, u32[]{:S(2)}) collective-permute-start(f32[3,1024,64]{1,2,0:T(8,128)S(1)} %get-tuple-element.154), channel_id=1, source_target_pairs={{16,0},{20,4},{24,8},{28,12},{32,16},{36,20},{40,24},{44,28},{48,3... | collective-permute-start | bytes 2359304 | tf_op jit(solution)/shard_map/ppermute | solution.py:10
  382.9 17.3 %collective-permute-start.7 = (f32[2,1024,64]{1,2,0:T(8,128)S(1)}, f32[2,1024,64]{1,2,0:T(8,128)S(1)}, u32[]{:S(2)}, u32[]{:S(2)}) collective-permute-start(f32[2,1024,64]{1,2,0:T(8,128)S(1)} %get-tuple-element.156), channel_id=1, source_target_pairs={{0,32},{4,36},{8,40},{12,44},{16,48},{20,52},{24,56},{28,60},{32,6... | collective-permute-start | bytes 1572872 | tf_op jit(solution)/shard_map/ppermute | solution.py:10
  390.9 16.5 %collective-permute-start.8 = (f32[2,1024,64]{1,2,0:T(8,128)S(1)}, f32[2,1024,64]{1,2,0:T(8,128)S(1)}, u32[]{:S(2)}, u32[]{:S(2)}) collective-permute-start(f32[2,1024,64]{1,2,0:T(8,128)S(1)} %get-tuple-element.156), channel_id=1, source_target_pairs={{32,0},{36,4},{40,8},{44,12},{48,16},{52,20},{56,24},{60,28},{64,3... | collective-permute-start | bytes 1572872 | tf_op jit(solution)/shard_map/ppermute | solution.py:10
  407.5 9.5 %copy-start.2 = (f32[512,256]{0,1:T(8,128)S(1)}, f32[512,256]{0,1:T(8,128)}, u32[]{:S(2)}) copy-start(f32[512,256]{0,1:T(8,128)} %reduce-scatter.3.cloned.1.call-done) | copy-start | bytes 1572868
  409.6 16.4 %collective-permute-start.10 = (f32[1,1024,64]{2,1,0:T(8,128)S(1)}, f32[1,1024,64]{2,1,0:T(8,128)S(1)}, u32[]{:S(2)}, u32[]{:S(2)}) collective-permute-start(f32[1,1024,64]{2,1,0:T(8,128)S(1)} %get-tuple-element.221), channel_id=1, source_target_pairs={{64,0},{68,4},{72,8},{76,12},{80,16},{84,20},{88,24},{92,28},{96,3... | collective-permute-start | bytes 786440 | tf_op jit(solution)/shard_map/ppermute | solution.py:10
  410.9 16.3 %collective-permute-start.9 = (f32[1,1024,64]{2,1,0:T(8,128)S(1)}, f32[1,1024,64]{2,1,0:T(8,128)S(1)}, u32[]{:S(2)}, u32[]{:S(2)}) collective-permute-start(f32[1,1024,64]{2,1,0:T(8,128)S(1)} %get-tuple-element.221), channel_id=1, source_target_pairs={{0,64},{4,68},{8,72},{12,76},{16,80},{20,84},{24,88},{28,92},{32,9... | collective-permute-start | bytes 786440 | tf_op jit(solution)/shard_map/ppermute | solution.py:10
  417.1 160.9 %copy-start.1 = (f32[512,256]{1,0:T(8,128)S(1)}, f32[512,256]{1,0:T(8,128)}, u32[]{:S(2)}) copy-start(f32[512,256]{1,0:T(8,128)} %param.20) | copy-start | bytes 1572868
Sparse Core Ops, SparseCore 0:
  43.6 33.2 reduce-scatter.2
  93.3 64.6 reduce-scatter.4
where the time goes:
time: 595 us; the launch traced here: 585 us
  waiting for transfers between devices  270 us (45%)
  blocking collectives  171 us (29%)
  matrix products  65.8 us (11%)
  starting transfers between devices  32.2 us (5%)
  between operations  14.6 us (2%)
  other arithmetic  11.5 us (2%)
  loops' own time  10.3 us (2%)
  local copies, waits for them, and re-layouts  9.81 us (2%)
    ppermute x11, waiting for transfers between devices, passed_along(): lax.ppermute(value, axis, [(source, source + steps) for source in range(i...  172 us
    psum x1, blocking collectives, local(): total = lax.psum(leaf_squares + placed, ('leaf', 'grid'))  149 us
    reduce_scatter x1, waiting for transfers between devices, local(): lax.psum_scatter(partial_update, 'grid', scatter_dimension=2, tiled=True)  64.9 us
    reduce_scatter x1, waiting for transfers between devices, local(): lax.psum_scatter(jnp.dot(leaf_inverse, local_rhs, precision=highest, pref...  33 us
    dot_general x5, matrix products, solve(): jnp.dot(own_panels[step], result, precision=highest, preferred_element_ty...  32.2 us
    ppermute x11, starting transfers between devices, passed_along(): lax.ppermute(value, axis, [(source, source + steps) for source in range(i...  31.9 us
    all_to_all x1, blocking collectives, local(): lax.all_to_all(picked.reshape(block_count, slots, columns), ('leaf', 'gri...  22.2 us
    dot_general x1, matrix products, local(): jnp.einsum('tsr,rk->tsk', masked, leaf_y, precision=highest)  16.4 us
  transfers between devices with their start and end apart: 13, of which 12 were waited for; matrix products, arithmetic and copies ran while one was open for 0% of the time, Pallas kernels for 0%

commit v1 on v0

v1 whole, which is shorter than its diff:
```python
import jax
import jax.numpy as jnp
from jax import lax
from jax.experimental import pallas as pl
from jax.experimental.pallas import tpu as pltpu
from jax.sharding import PartitionSpec as P

F32, BF16 = jnp.float32, jnp.bfloat16
MESH = pl.DeviceIdType.MESH
DMA = pltpu.SemaphoreType.DMA


def split(value):
    high = value.astype(BF16)
    return high, (value - high.astype(F32)).astype(BF16)


def dot(a, b):
    return jnp.dot(a, b, preferred_element_type=F32)


def dot3(a, b_high, b_low):
    high, low = split(a)
    return dot(high, b_high) + dot(high, b_low) + dot(low, b_high)


def lane_left(shape):
    return lax.broadcasted_iota(jnp.int32, shape, 1) < 64


def turned(value):
    return pltpu.roll(value, 64, 1)


def packed_pair(top, bottom):
    left = lane_left(top.shape)
    return jnp.where(left, top, turned(bottom)), jnp.where(left, turned(top), bottom)


def unpacked(value):
    left = lane_left(value.shape)
    other = turned(value)
    return jnp.where(left, value, other), jnp.where(left, other, value)


def rows(start, size, unit=8):
    if isinstance(start, int):
        return pl.ds(start, size)
    return pl.ds(pl.multiple_of(start, unit), size)


def kernel(order_ref, mask_ref, rhs_ref, linv_hbm, lpan_hbm, srhs_hbm, sinv_hbm, span_hbm,
           leafy_hbm, sol_hbm, width_ref,
           abuf, xbuf, xh, xl, lbuf, zs, zr, za, ybuf, yh_s, yl_s, pbuf, own, snd, rcv, zrs,
           pk12, pk3, ubuf, accp, pend, rhsv, rhsp, vcat, vh0, solv, invb, spb, csend, crecv, wsend, wrecv,
           ld_sem, lp_sem, sp_sem, a2a_sem, zs_sem, zr_sem, za_sem, us_sem, ur_sem, rs_sem, rr_sem,
           ps_sem, p3_sem, u_sem, cs_sem, cr_sem, w_sem, out_sem):
    leaf = lax.axis_index("leaf")
    grid = lax.axis_index("grid")
    me = leaf * 4 + grid
    yl = lax.rem(leaf, 2)
    z = lax.rem(lax.div(leaf, 2), 4)
    x = lax.div(leaf, 8)
    yh = lax.div(grid, 2)
    c = lax.rem(grid, 2)
    sib = yh * 2 + 1 - c

    level = jnp.int32(1)
    for bit in range(1, 6):
        level = level + (lax.rem(leaf + 1, 2 ** bit) == 0).astype(jnp.int32)
    parent = jnp.int32(0)
    for tier in range(1, 6):
        size = 2 ** (tier + 1)
        parent = jnp.where(level == tier, lax.div(leaf, size) * size + 2 ** tier - 1, parent)
    side = (leaf > parent).astype(jnp.int32)
    n_pan = 6 - level

    l_copy = pltpu.make_async_copy(linv_hbm, lbuf, ld_sem.at[0])
    l_copy.start()
    inv_copy = pltpu.make_async_copy(sinv_hbm, invb, ld_sem.at[1])
    srhs_copy = pltpu.make_async_copy(srhs_hbm, rhsv, ld_sem.at[2])

    def lp_copy(t):
        return pltpu.make_async_copy(lpan_hbm.at[t], pbuf.at[t % 3], lp_sem.at[t % 3])

    def sp_copy(m):
        slot = lax.rem(m, 3)
        return pltpu.make_async_copy(span_hbm.at[m], spb.at[slot], sp_sem.at[slot])

    rh, rl = split(rhs_ref[...])
    for part in range(4):
        index = order_ref[rows(part * 256, 256), :]
        hot = (lax.broadcasted_iota(jnp.int32, (256, 512), 1) == index).astype(BF16)
        got = dot(hot, rh) + dot(hot, rl)
        upper = lax.rem(lax.broadcasted_iota(jnp.int32, (256, 128), 0), 8) < 4
        abuf[rows(part * 256, 256), :] = jnp.where(upper, got[:, :128], got[:, 128:])

    barrier = pltpu.get_barrier_semaphore()

    def greet(k, carry):
        d = lax.rem(me + k, 128)
        pl.semaphore_signal(barrier, inc=1, device_id=(lax.div(d, 4), lax.rem(d, 4)), device_id_type=MESH)
        return carry

    lax.fori_loop(1, 128, greet, 0)
    for t in range(3):
        lp_copy(t).start()
    srhs_copy.start()
    pl.semaphore_wait(barrier, 127)

    def a2a(k, carry):
        d = lax.rem(me + k, 128)
        pltpu.make_async_remote_copy(
            src_ref=abuf.at[rows(d * 8, 8)], dst_ref=xbuf.at[rows(me * 8, 8)],
            send_sem=a2a_sem.at[0], recv_sem=a2a_sem.at[1],
            device_id=(lax.div(d, 4), lax.rem(d, 4)), device_id_type=MESH).start()
        return carry

    lax.fori_loop(1, 128, a2a, 0)
    xbuf[rows(me * 8, 8), :] = abuf[rows(me * 8, 8), :]
    inv_copy.start()
    for m in range(3):
        @pl.when(m < n_pan)
        def _():
            sp_copy(jnp.int32(m)).start()
    pltpu.make_async_copy(xbuf.at[pl.ds(0, 1016)], xbuf.at[pl.ds(0, 1016)], a2a_sem.at[1]).wait()

    raw = xbuf[...].reshape(64, 2, 8, 128)
    first, second = raw[:, 0], raw[:, 1]
    upper = lax.broadcasted_iota(jnp.int32, (64, 8, 128), 1) < 4
    left = jnp.where(upper, first, pltpu.roll(second, 4, 1)).reshape(512, 128)
    right = jnp.where(upper, pltpu.roll(first, 4, 1), second).reshape(512, 128)
    for half, value in enumerate((left, right)):
        high, low = split(value)
        xh[:, half * 128:(half + 1) * 128] = high
        xl[:, half * 128:(half + 1) * 128] = low

    l_copy.wait()

    def leaf_block(r, dst):
        def body(i, carry):
            dst[rows(i * 256, 256), :] = dot3(lbuf[rows(r * 512 + i * 256, 256), :], xh[...], xl[...])
            return carry
        lax.fori_loop(0, 2, body, 0)

    def to_sibling(slot):
        return pltpu.make_async_remote_copy(
            src_ref=zs.at[slot], dst_ref=zr.at[slot], send_sem=zs_sem.at[slot], recv_sem=zr_sem.at[slot],
            device_id=(leaf, sib), device_id_type=MESH)

    def across():
        return pltpu.make_async_remote_copy(
            src_ref=zs.at[2], dst_ref=za, send_sem=zs_sem.at[2], recv_sem=za_sem,
            device_id=(leaf, 2 + c), device_id_type=MESH)

    @pl.when(yh == 0)
    def _():
        leaf_block(3 - c, zs.at[0])
        to_sibling(0).start()
        leaf_block(2 + c, zs.at[2])
        to_sibling(0).wait_recv()
        zs[2] = zs[2] + zr[0]
        across().start()

        @pl.when(c == 0)
        def _():
            leaf_block(1, zs.at[1])
            to_sibling(1).start()

    @pl.when((yh == 1) & (c == 0))
    def _():
        leaf_block(3, zs.at[1])
        to_sibling(1).start()

    leaf_block(grid, ybuf)

    @pl.when(c == 1)
    def _():
        to_sibling(1).wait_recv()
        ybuf[...] = ybuf[...] + zr[1]

    @pl.when(yh == 1)
    def _():
        across().wait_recv()
        ybuf[...] = ybuf[...] + za[...]

    y_out = pltpu.make_async_copy(ybuf, leafy_hbm, out_sem.at[0])
    y_out.start()

    y_left, y_right = ybuf[:, :128], ybuf[:, 128:]
    for_0, for_1 = packed_pair(y_left, y_right)
    mine = jnp.where(c == 0, for_0, for_1)
    other = jnp.where(c == 0, for_1, for_0)
    own[0, pl.ds(1024, 8), :] = jnp.broadcast_to(jnp.sum(mine * mine, axis=0, keepdims=True), (8, 128))
    snd[0, pl.ds(1024, 8), :] = jnp.broadcast_to(jnp.sum(other * other, axis=0, keepdims=True), (8, 128))
    for half, value in enumerate((mine, other)):
        high, low = split(value)
        yh_s[:, half * 128:(half + 1) * 128] = high
        yl_s[:, half * 128:(half + 1) * 128] = low

    def u_copy(t):
        size = 1032 if t == 0 else 1024
        return pltpu.make_async_remote_copy(
            src_ref=snd.at[t, pl.ds(0, size)], dst_ref=rcv.at[t, pl.ds(0, size)],
            send_sem=us_sem.at[t], recv_sem=ur_sem.at[t], device_id=(leaf, sib), device_id_type=MESH)

    def send_pieces(src, base, size, to_leaf, sems, recv_sem):
        for to_yh in range(2):
            to_me = (to_leaf == leaf) & (yh == to_yh)

            @pl.when(to_me)
            def _():
                ubuf[rows(base, size), :] = src[to_yh]

            @pl.when(jnp.logical_not(to_me))
            def _():
                pltpu.make_async_remote_copy(
                    src_ref=src.at[to_yh], dst_ref=ubuf.at[rows(base, size)],
                    send_sem=sems.at[to_yh], recv_sem=recv_sem,
                    device_id=(to_leaf, to_yh * 2 + c), device_id_type=MESH).start()

    def wait_pieces(src, base, size, to_leaf, sems):
        for to_yh in range(2):
            @pl.when(jnp.logical_not((to_leaf == leaf) & (yh == to_yh)))
            def _():
                pltpu.make_async_copy(src.at[to_yh], src.at[to_yh], sems.at[to_yh]).wait()

    y_src = yl * 2 + yh
    leaf_1 = leaf - yl
    leaf_2 = (x * 4 + z - lax.rem(z, 2)) * 2 + 1
    leaf_3 = x * 8 + 3
    piece_1 = (pk12.at[0], y_src * 520, 520, leaf_1, ps_sem.at[0])
    piece_2 = (pk12.at[1, :, pl.ds(0, 512)], (lax.rem(z, 2) * 4 + y_src) * 512, 512, leaf_2, ps_sem.at[1])

    def piece_3(t):
        return (pk3.at[t - 2], ((t - 2) * 16 + y_src * 4 + z) * 128, 128, leaf_3, p3_sem.at[t - 2])

    def rs_copy(t, k):
        q = lax.rem(z + k, 4)
        return pltpu.make_async_remote_copy(
            src_ref=own.at[t, rows(q * 256, 256)], dst_ref=zrs.at[t - 2, 3 - k],
            send_sem=rs_sem.at[t - 2, k - 1], recv_sem=rr_sem.at[t - 2, 3 - k],
            device_id=((x * 4 + q) * 2 + yl, grid), device_id_type=MESH)

    def spread(t):
        u_copy(t).wait_recv()
        if t < 2:
            def body(i, carry):
                base = i * 256
                top = own[t, rows(base, 128), :] + rcv[t, rows(base, 128), :]
                bottom = own[t, rows(base + 128, 128), :] + rcv[t, rows(base + 128, 128), :]
                p0, p1 = packed_pair(top, bottom)
                pk12[t, 0, rows(i * 128, 128), :] = p0
                pk12[t, 1, rows(i * 128, 128), :] = p1
                return carry
            lax.fori_loop(0, 4, body, 0)
            if t == 0:
                squares = own[0, pl.ds(1024, 8), :] + rcv[0, pl.ds(1024, 8), :]
                pk12[0, 0, pl.ds(512, 8), :] = squares
                pk12[0, 1, pl.ds(512, 8), :] = turned(squares)
            send_pieces(*(piece_1 if t == 0 else piece_2), u_sem.at[0])
        else:
            def body(i, carry):
                part = rows(i * 256, 256)
                own[t, part, :] = own[t, part, :] + rcv[t, part, :]
                return carry
            lax.fori_loop(0, 4, body, 0)
            for k in range(1, 4):
                rs_copy(t, k).start()

    for t in range(6):
        lp_copy(t).wait()
        masks = [mask_ref[pl.ds(t * 4 + b, 1), :] for b in range(4)]
        masked = lambda ref: jnp.concatenate(
            [ref[b * 128:(b + 1) * 128, :] * jnp.concatenate([masks[b]] * 2, axis=1) for b in range(4)], axis=0)
        y_high, y_low = masked(yh_s), masked(yl_s)
        xh[...] = y_high
        xl[...] = y_low

        def body(i, carry):
            part = rows(i * 256, 256)
            product = dot3(pbuf[t % 3, part, :], xh[...], xl[...])
            own[t, part, :] = product[:, :128]
            snd[t, part, :] = product[:, 128:]
            return carry
        lax.fori_loop(0, 4, body, 0)
        if t + 3 < 6:
            lp_copy(t + 3).start()
        u_copy(t).start()
        if t > 0:
            spread(t - 1)
    spread(5)

    def gather_rs(t):
        for k in range(1, 4):
            rs_copy(t, k).wait_recv()
        base = z * 256

        def total(start):
            value = own[t, rows(base + start, 128), :]
            for k in range(3):
                value = value + zrs[t - 2, k, pl.ds(start, 128), :]
            return value
        p0, p1 = packed_pair(total(0), total(128))
        pk3[t - 2, 0] = p0
        pk3[t - 2, 1] = p1
        send_pieces(*piece_3(t), u_sem.at[t - 2])

    def up_copy(m, size):
        return pltpu.make_async_remote_copy(
            src_ref=csend.at[m, pl.ds(0, size)], dst_ref=crecv.at[side, m, pl.ds(0, size)],
            send_sem=cs_sem.at[m], recv_sem=cr_sem.at[side, m], device_id=(parent, grid), device_id_type=MESH)

    def wait_child(s, m, size):
        pltpu.make_async_copy(csend.at[m, pl.ds(0, size)], crecv.at[s, m, pl.ds(0, size)], cr_sem.at[s, m]).wait()

    def take_3(k, dst):
        start = k * 2048
        pltpu.make_async_copy(ubuf.at[pl.ds(0, 1920)], ubuf.at[pl.ds(0, 1920)], u_sem.at[k]).wait()
        value = ubuf[rows(start, 512), :]
        for s in range(1, 4):
            value = value + ubuf[rows(start + s * 512, 512), :]
        dst[pl.ds(0, 512), :] = dst[pl.ds(0, 512), :] + value

    def chain():
        accp[...] = jnp.zeros_like(accp)

        @pl.when(level == 1)
        def _():
            pltpu.make_async_copy(ubuf.at[pl.ds(0, 1560)], ubuf.at[pl.ds(0, 1560)], u_sem.at[0]).wait()
            accp[...] = ubuf[0:520, :] + ubuf[520:1040, :] + ubuf[1040:1560, :] + ubuf[1560:2080, :]

        @pl.when(level == 2)
        def _():
            pltpu.make_async_copy(ubuf.at[pl.ds(0, 3584)], ubuf.at[pl.ds(0, 3584)], u_sem.at[0]).wait()
            value = ubuf[0:512, :]
            for s in range(1, 8):
                value = value + ubuf[s * 512:(s + 1) * 512, :]
            accp[0:512, :] = value

        @pl.when(level == 3)
        def _():
            take_3(0, accp)

        @pl.when(level > 1)
        def _():
            wait_child(0, 0, 520)
            accp[...] = accp[...] + crecv[0, 0]

        @pl.when((level > 1) & (level < 6))
        def _():
            wait_child(1, 0, 520)
            accp[...] = accp[...] + crecv[1, 0]

        for i in range(4):
            left = lane_left((128, 128))
            for j, value in enumerate(unpacked(accp[i * 128:(i + 1) * 128, :])):
                part = pl.ds(i * 256 + j * 128, 128)
                right_side = rhsp[part, :]
                v = jnp.where(left, right_side, turned(right_side)) - value
                high, low = split(v)
                vcat[0, part, :] = jnp.where(left, high.astype(F32), low.astype(F32)).astype(BF16)
                vh0[0, part, :] = jnp.where(left, high.astype(F32), 0.0).astype(BF16)
        squares = accp[512:520, :]
        for r in range(4):
            part = pl.ds(r * 256, 256)
            depth = (r + 1) * 256
            high, low = split(invb[part, 0:depth])
            product = dot(high, vcat[0, 0:depth, :]) + dot(low, vh0[0, 0:depth, :])
            s_value = product + turned(product)
            solv[part, :] = s_value[:, :64]
            left = lane_left((256, 128))
            high, low = split(s_value)
            vcat[1, part, :] = jnp.where(left, high.astype(F32), low.astype(F32)).astype(BF16)
            vh0[1, part, :] = jnp.where(left, high.astype(F32), 0.0).astype(BF16)
            squares = squares + jnp.sum(s_value * s_value, axis=0, keepdims=True)
        csend[0, pl.ds(512, 8), :] = squares
        pltpu.make_async_copy(solv, sol_hbm, out_sem.at[1]).start()

        def panel(m, carry):
            sp_copy(m).wait()
            pend[...] = jnp.zeros_like(pend)

            @pl.when(level > 1)
            def _():
                wait_child(0, m + 1, 512)
                wait_child(1, m + 1, 512)
                pend[...] = crecv[0, m + 1, 0:512, :] + crecv[1, m + 1, 0:512, :]

            @pl.when(level == 3)
            def _():
                take_3(m + 1, pend)

            slot = lax.rem(m, 3)

            def body(i, inner):
                high, low = split(spb[slot, rows(i * 256, 256), :])
                product = dot(high, vcat[1]) + dot(low, vh0[1])
                total = product + turned(product)
                left = lane_left((128, 128))
                part = rows(i * 128, 128)
                csend[m, part, :] = jnp.where(left, total[:128], total[128:]) + pend[part, :]
                return inner
            lax.fori_loop(0, 4, body, 0)

            @pl.when(m == 0)
            def _():
                up_copy(m, 520).start()

            @pl.when(m > 0)
            def _():
                up_copy(m, 512).start()

            @pl.when(m + 3 < n_pan)
            def _():
                sp_copy(m + 3).start()
            return carry
        lax.fori_loop(0, n_pan, panel, 0)

    srhs_copy.wait()
    rhsp[...] = jnp.zeros_like(rhsp)
    rhsp[:, :64] = rhsv[...]
    inv_copy.wait()

    turn = jnp.minimum(level, 3) - 1

    def phase(p, carry):
        @pl.when(p == turn)
        def _():
            chain()

        @pl.when(p == 0)
        def _():
            gather_rs(2)
            gather_rs(3)

        @pl.when(p == 1)
        def _():
            gather_rs(4)
            gather_rs(5)
        return carry
    lax.fori_loop(0, 3, phase, 0)

    def width_copy(d):
        return pltpu.make_async_remote_copy(
            src_ref=wsend, dst_ref=wrecv, send_sem=w_sem.at[0], recv_sem=w_sem.at[1],
            device_id=(d, grid), device_id_type=MESH)

    @pl.when(level == 6)
    def _():
        wsend[0] = jnp.sqrt(csend[0, pl.ds(512, 8), :] / (32 * 3072) + 1e-06)
        for d in range(31):
            width_copy(d).start()
        width_ref[...] = wsend[0]
        pltpu.make_async_copy(abuf.at[pl.ds(0, 248)], abuf.at[pl.ds(0, 248)], w_sem.at[0]).wait()

    @pl.when(level < 6)
    def _():
        width_copy(0).wait_recv()
        width_ref[...] = wrecv[0]

    pltpu.make_async_copy(abuf.at[pl.ds(0, 1016)], abuf.at[pl.ds(0, 1016)], a2a_sem.at[0]).wait()

    @pl.when(yh == 0)
    def _():
        to_sibling(0).wait_send()
        across().wait_send()

    @pl.when(c == 0)
    def _():
        to_sibling(1).wait_send()
    y_out.wait()
    pltpu.make_async_copy(solv, sol_hbm, out_sem.at[1]).wait()
    for t in range(6):
        u_copy(t).wait_send()
    wait_pieces(*piece_1)
    wait_pieces(*piece_2)
    for t in range(2, 6):
        for k in range(1, 4):
            rs_copy(t, k).wait_send()
        wait_pieces(*piece_3(t))

    def sent(m, carry):
        @pl.when(m == 0)
        def _():
            up_copy(m, 520).wait_send()

        @pl.when(m > 0)
        def _():
            up_copy(m, 512).wait_send()
        return carry
    lax.fori_loop(0, n_pan, sent, 0)


def local(rhs_rows, order, leaf_inverse, leaf_panels, panel_mask, sep_rhs, sep_inverse, sep_panels):
    twice = jnp.broadcast_to(order.reshape(128, 1, 4), (128, 2, 4)).reshape(1024, 1)
    mask = jnp.broadcast_to(panel_mask.reshape(24, 1).astype(BF16), (24, 128))
    vmem = pl.BlockSpec(memory_space=pltpu.VMEM)
    hbm = pl.BlockSpec(memory_space=pl.ANY)
    V = pltpu.VMEM
    leaf_y, solved, width = pl.pallas_call(
        kernel,
        out_shape=(
            jax.ShapeDtypeStruct((512, 256), F32),
            jax.ShapeDtypeStruct((1024, 64), F32),
            jax.ShapeDtypeStruct((8, 128), F32),
        ),
        in_specs=[vmem] * 3 + [hbm] * 5,
        out_specs=(hbm, hbm, vmem),
        scratch_shapes=[
            V((1024, 128), F32), V((1024, 128), F32),
            V((512, 256), BF16), V((512, 256), BF16),
            V((2048, 512), F32),
            V((3, 512, 256), F32), V((2, 512, 256), F32), V((512, 256), F32),
            V((512, 256), F32), V((512, 256), BF16), V((512, 256), BF16),
            V((3, 1024, 512), F32),
            V((6, 1032, 128), F32), V((6, 1032, 128), F32), V((6, 1032, 128), F32),
            V((4, 3, 256, 128), F32),
            V((2, 2, 520, 128), F32), V((4, 2, 128, 128), F32),
            V((8192, 128), F32),
            V((520, 128), F32), V((512, 128), F32),
            V((1024, 64), F32), V((1024, 128), F32),
            V((2, 1024, 128), BF16), V((2, 1024, 128), BF16),
            V((1024, 64), F32),
            V((1024, 1024), F32), V((3, 1024, 1024), F32),
            V((5, 520, 128), F32), V((2, 5, 520, 128), F32),
            V((1, 8, 128), F32), V((1, 8, 128), F32),
            DMA((3,)), DMA((3,)), DMA((3,)), DMA((2,)), DMA((3,)), DMA((2,)), DMA, DMA((6,)), DMA((6,)),
            DMA((4, 3)), DMA((4, 3)), DMA((2, 2)), DMA((4, 2)), DMA((4,)), DMA((5,)), DMA((2, 5)), DMA((2,)), DMA((2,)),
        ],
        compiler_params=pltpu.CompilerParams(
            collective_id=0, has_side_effects=True, vmem_limit_bytes=62 * 2 ** 20),
        cost_estimate=pl.CostEstimate(flops=7 * 10 ** 9, bytes_accessed=44 * 10 ** 6, transcendentals=0),
    )(twice, mask, rhs_rows, leaf_inverse, leaf_panels[0], sep_rhs[0], sep_inverse[0], sep_panels[0])
    return leaf_y, solved[None], width[0, :64]


def solution(mesh):
    placed = (
        P(("leaf", "grid"), None),
        P(("leaf", "grid")),
        P("leaf", "grid"),
        P("leaf", None, None, "grid"),
        P("leaf", None, "grid"),
        P("leaf", None, "grid"),
        P("leaf", None, None),
        P("leaf", None, None, None),
    )
    return jax.shard_map(
        local,
        mesh=mesh,
        in_specs=placed,
        out_specs=(P(("leaf", "grid"), None), P("leaf", None, "grid"), P("grid")),
        check_vma=False,
    )
```

time: 595 us -> 224 us (0.38); the launches traced: 585 us -> 223 us
  waiting for transfers between devices: 270 us -> 0 us
  Pallas kernels: 0 us -> 212 us
  blocking collectives: 171 us -> 0 us
  matrix products: 65.8 us -> 0 us
  starting transfers between devices: 32.2 us -> 0 us
  between operations: 14.6 us -> 0.66 us
  other arithmetic: 11.5 us -> 0.69 us
  loops' own time: 10.3 us -> 0 us
    pallas_call x0 -> x1, Pallas kernels: none -> 212 us  [local(): pl.pallas_call(kernel, out_shape=(jax.ShapeDtypeStruct((512, 256), F32),...]
    ppermute x11 -> x0, waiting for transfers between devices: 172 us -> none  [passed_along(): lax.ppermute(value, axis, [(source, source + steps) for source in range(i...]
    psum x1 -> x0, blocking collectives: 149 us -> none  [local(): total = lax.psum(leaf_squares + placed, ('leaf', 'grid'))]
    reduce_scatter x2 -> x0, waiting for transfers between devices: 97.8 us -> none  [the longest x1 64.9 us: local(): lax.psum_scatter(partial_update, 'grid', scatter_dimension=2, tiled=True)]
    dot_general x8 -> x0, matrix products: 65.8 us -> none  [the longest x5 32.2 us: solve(): jnp.dot(own_panels[step], result, precision=highest, preferred_element_ty...]
    ppermute x11 -> x0, starting transfers between devices: 31.9 us -> none  [passed_along(): lax.ppermute(value, axis, [(source, source + steps) for source in range(i...]
    all_to_all x1 -> x0, blocking collectives: 22.2 us -> none  [local(): lax.all_to_all(picked.reshape(block_count, slots, columns), ('leaf', 'gri...]
    another operation x6 -> x0, loops' own time: 10.3 us -> none  [local(): tail, solved = lax.cond(is_host, solve, keep, (tail, solved))]
  transfers between devices with their start and end apart: 13 -> 0, of which waited for: 12 -> 0; matrix products, arithmetic and copies ran while one was open for 0% -> 0% of each run, Pallas kernels for 0% -> 0%
where the time goes in v1:
time: 224 us; the launch traced here: 223 us
  Pallas kernels  212 us (95%)
  local copies, waits for them, and re-layouts  9.66 us (4%)
    pallas_call x1, Pallas kernels, local(): pl.pallas_call(kernel, out_shape=(jax.ShapeDtypeStruct((512, 256), F32),...  212 us
    unnamed x3, local copies, waits for them, and re-layouts  5.73 us

profile of v1, /device:TPU:16, one launch (start us, length us, event | category | flops | bytes accessed | tf_op | source)
XLA Modules:
  0.0 223.2 jit_solution(1406592336642728419)
XLA Ops:
  0.6 0.7 convert_element_type.11
  1.3 0.1 copy.14
  1.4 0.1 convert_element_type.12
  1.5 0.7 broadcast_in_dim.17.mask_ref
  2.2 0.8 broadcast_in_dim.15
  3.0 1.0 reshape.21.order_ref
  4.1 1.9 copy.15
  6.0 212.2 %shard_map.103 = (f32[512,256]{1,0:T(8,128)}, f32[1024,64]{1,0:T(8,128)}, f32[8,128]{1,0:T(8,128)}) custom-call(s32[1024,1]{1,0:T(8,128)} %reshape.21.order_ref, bf16[24,128]{1,0:T(8,128)(2,1)} %broadcast_in_dim.17.mask_ref, f32[512,256]{1,0:T(8,128)} %rhs_ref.1, f32[2048,512]{1,0:T(8,128)} %linv_hbm.1, f32[6,1024,512]{2,1,0:T(8,128)} %bitcast.8, ...), custom_call_target="tpu_custom_call" | custom-call | flops 7000000000 | bytes 44000000 | tf_op jit(solution)/shard_map/pallas_call | solution.py:501
  218.2 1.9 copy.17
  220.2 1.2 slice_bitcast_fusion
  221.4 1.9 copy.19
  (1 shorter events, 0.0 us)

commit v2 on v1

--- a/solution.py
+++ b/solution.py
@@ -52,7 +52,7 @@
 def kernel(order_ref, mask_ref, rhs_ref, linv_hbm, lpan_hbm, srhs_hbm, sinv_hbm, span_hbm,
            leafy_hbm, sol_hbm, width_ref,
            abuf, xbuf, xh, xl, lbuf, zs, zr, za, ybuf, yh_s, yl_s, pbuf, own, snd, rcv, zrs,
-           pk12, pk3, ubuf, accp, pend, rhsv, rhsp, vcat, vh0, solv, invb, spb, csend, crecv, wsend, wrecv,
+           pk12, pk3, ubuf, accp, pend, squares, cacc, racc, rhsv, rhsp, vcat, vh0, solv, invb, spb, csend, crecv, wsend, wrecv,
            ld_sem, lp_sem, sp_sem, a2a_sem, zs_sem, zr_sem, za_sem, us_sem, ur_sem, rs_sem, rr_sem,
            ps_sem, p3_sem, u_sem, cs_sem, cr_sem, w_sem, out_sem):
     leaf = lax.axis_index("leaf")
@@ -88,12 +88,16 @@
         return pltpu.make_async_copy(span_hbm.at[m], spb.at[slot], sp_sem.at[slot])
 
     rh, rl = split(rhs_ref[...])
+    index = order_ref[...].astype(F32)
+    index = jnp.transpose(jnp.concatenate([index, index], axis=0)).astype(jnp.int32)
+    upper = lax.broadcasted_iota(jnp.int32, (16, 8, 128), 1) < 4
     for part in range(4):
-        index = order_ref[rows(part * 256, 256), :]
-        hot = (lax.broadcasted_iota(jnp.int32, (256, 512), 1) == index).astype(BF16)
+        hot = (lax.broadcasted_iota(jnp.int32, (128, 512), 1) == index[:, part:part + 1]).astype(F32).astype(BF16)
         got = dot(hot, rh) + dot(hot, rl)
-        upper = lax.rem(lax.broadcasted_iota(jnp.int32, (256, 128), 0), 8) < 4
-        abuf[rows(part * 256, 256), :] = jnp.where(upper, got[:, :128], got[:, 128:])
+        first, second = got[:, :128].reshape(16, 8, 128), got[:, 128:].reshape(16, 8, 128)
+        even = jnp.where(upper, first, pltpu.roll(second, 4, 1))
+        odd = jnp.where(upper, pltpu.roll(first, 4, 1), second)
+        abuf[rows(part * 256, 256), :] = jnp.stack([even, odd], axis=1).reshape(256, 128)
 
     barrier = pltpu.get_barrier_semaphore()
 
@@ -236,11 +240,13 @@
         return (pk3.at[t - 2], ((t - 2) * 16 + y_src * 4 + z) * 128, 128, leaf_3, p3_sem.at[t - 2])
 
     def rs_copy(t, k):
-        q = lax.rem(z + k, 4)
+        at = z if t < 4 else x
+        q = lax.rem(at + k, 4)
+        to_leaf = (x * 4 + q) * 2 + yl if t < 4 else (q * 4 + z) * 2 + yl
         return pltpu.make_async_remote_copy(
             src_ref=own.at[t, rows(q * 256, 256)], dst_ref=zrs.at[t - 2, 3 - k],
             send_sem=rs_sem.at[t - 2, k - 1], recv_sem=rr_sem.at[t - 2, 3 - k],
-            device_id=((x * 4 + q) * 2 + yl, grid), device_id_type=MESH)
+            device_id=(to_leaf, grid), device_id_type=MESH)
 
     def spread(t):
         u_copy(t).wait_recv()
@@ -270,9 +276,9 @@
 
     for t in range(6):
         lp_copy(t).wait()
-        masks = [mask_ref[pl.ds(t * 4 + b, 1), :] for b in range(4)]
+        masks = [jnp.full((1, 256), mask_ref[t, b].astype(F32)).astype(BF16) for b in range(4)]
         masked = lambda ref: jnp.concatenate(
-            [ref[b * 128:(b + 1) * 128, :] * jnp.concatenate([masks[b]] * 2, axis=1) for b in range(4)], axis=0)
+            [ref[b * 128:(b + 1) * 128, :] * masks[b] for b in range(4)], axis=0)
         y_high, y_low = masked(yh_s), masked(yl_s)
         xh[...] = y_high
         xl[...] = y_low
@@ -292,9 +298,9 @@
     spread(5)
 
     def gather_rs(t):
-        for k in range(1, 4):
-            rs_copy(t, k).wait_recv()
-        base = z * 256
+        for k in range(3):
+            pltpu.make_async_copy(zrs.at[t - 2, k], zrs.at[t - 2, k], rr_sem.at[t - 2, k]).wait()
+        base = jnp.where(t < 4, z, x) * 256
 
         def total(start):
             value = own[t, rows(base + start, 128), :]
@@ -306,29 +312,68 @@
         pk3[t - 2, 1] = p1
         send_pieces(*piece_3(t), u_sem.at[t - 2])
 
-    def up_copy(m, size):
+    def up_copy(m, i, size):
+        part = rows(i * 128, size)
         return pltpu.make_async_remote_copy(
-            src_ref=csend.at[m, pl.ds(0, size)], dst_ref=crecv.at[side, m, pl.ds(0, size)],
-            send_sem=cs_sem.at[m], recv_sem=cr_sem.at[side, m], device_id=(parent, grid), device_id_type=MESH)
-
-    def wait_child(s, m, size):
-        pltpu.make_async_copy(csend.at[m, pl.ds(0, size)], crecv.at[s, m, pl.ds(0, size)], cr_sem.at[s, m]).wait()
+            src_ref=csend.at[m, part], dst_ref=crecv.at[side, m, part],
+            send_sem=cs_sem.at[m, i], recv_sem=cr_sem.at[side, m, i], device_id=(parent, grid), device_id_type=MESH)
+
+    def wait_child(s, m, i, size):
+        part = rows(i * 128, size)
+        pltpu.make_async_copy(csend.at[m, part], crecv.at[s, m, part], cr_sem.at[s, m, i]).wait()
 
     def take_3(k, dst):
         start = k * 2048
         pltpu.make_async_copy(ubuf.at[pl.ds(0, 1920)], ubuf.at[pl.ds(0, 1920)], u_sem.at[k]).wait()
-        value = ubuf[rows(start, 512), :]
-        for s in range(1, 4):
-            value = value + ubuf[rows(start + s * 512, 512), :]
-        dst[pl.ds(0, 512), :] = dst[pl.ds(0, 512), :] + value
-
-    def chain():
-        accp[...] = jnp.zeros_like(accp)
+
+        @pl.when(k < 2)
+        def _():
+            value = ubuf[rows(start, 512), :]
+            for s in range(1, 4):
+                value = value + ubuf[rows(start + s * 512, 512), :]
+            dst[...] = value
+
+        @pl.when(k >= 2)
+        def _():
+            value = ubuf[rows(start, 128), :]
+            for s in range(1, 16):
+                value = value + ubuf[rows(start + s * 128, 128), :]
+            dst[...] = jnp.zeros_like(dst)
+            dst[rows(x * 128, 128), :] = value
+
+    def dot2(a, which, part):
+        high, low = split(a)
+        return dot(high, vcat[which, part, :]) + dot(low, vh0[which, part, :])
+
+    def stacked(value, which, part):
+        left = lane_left(value.shape)
+        high, low = split(value)
+        vcat[which, part, :] = jnp.where(left, high.astype(F32), low.astype(F32)).astype(BF16)
+        vh0[which, part, :] = jnp.where(left, high.astype(F32), 0.0).astype(BF16)
+
+    def finished(product, m, i):
+        total = product + turned(product)
+        part = rows(i * 128, 128)
+        csend[m, part, :] = jnp.where(lane_left((128, 128)), total[:128], total[128:])
+
+        @pl.when(level == 3)
+        def _():
+            csend[m, part, :] = csend[m, part, :] + pend[part, :]
+
+        @pl.when(level > 1)
+        def _():
+            wait_child(0, m + 1, i, 128)
+            wait_child(1, m + 1, i, 128)
+            csend[m, part, :] = csend[m, part, :] + (crecv[0, m + 1, part, :] + crecv[1, m + 1, part, :])
+
+    def head():
+        squares[...] = jnp.zeros_like(squares)
 
         @pl.when(level == 1)
         def _():
             pltpu.make_async_copy(ubuf.at[pl.ds(0, 1560)], ubuf.at[pl.ds(0, 1560)], u_sem.at[0]).wait()
-            accp[...] = ubuf[0:520, :] + ubuf[520:1040, :] + ubuf[1040:1560, :] + ubuf[1560:2080, :]
+            accp[...] = ubuf[0:512, :] + ubuf[520:1032, :] + ubuf[1040:1552, :] + ubuf[1560:2072, :]
+            squares[...] = ubuf[512:520, :] + ubuf[1032:1040, :] + ubuf[1552:1560, :] + ubuf[2072:2080, :]
 
         @pl.when(level == 2)
         def _():
@@ -336,110 +381,115 @@
             value = ubuf[0:512, :]
             for s in range(1, 8):
                 value = value + ubuf[s * 512:(s + 1) * 512, :]
-            accp[0:512, :] = value
+            accp[...] = value
 
         @pl.when(level == 3)
         def _():
             take_3(0, accp)
-
-        @pl.when(level > 1)
-        def _():
-            wait_child(0, 0, 520)
-            accp[...] = accp[...] + crecv[0, 0]
-
-        @pl.when((level > 1) & (level < 6))
-        def _():
-            wait_child(1, 0, 520)
-            accp[...] = accp[...] + crecv[1, 0]
-
-        for i in range(4):
-            left = lane_left((128, 128))
-            for j, value in enumerate(unpacked(accp[i * 128:(i + 1) * 128, :])):
-                part = pl.ds(i * 256 + j * 128, 128)
-                right_side = rhsp[part, :]
-                v = jnp.where(left, right_side, turned(right_side)) - value
-                high, low = split(v)
-                vcat[0, part, :] = jnp.where(left, high.astype(F32), low.astype(F32)).astype(BF16)
-                vh0[0, part, :] = jnp.where(left, high.astype(F32), 0.0).astype(BF16)
-        squares = accp[512:520, :]
-        for r in range(4):
-            part = pl.ds(r * 256, 256)
-            depth = (r + 1) * 256
-            high, low = split(invb[part, 0:depth])
-            product = dot(high, vcat[0, 0:depth, :]) + dot(low, vh0[0, 0:depth, :])
-            s_value = product + turned(product)
-            solv[part, :] = s_value[:, :64]
-            left = lane_left((256, 128))
-            high, low = split(s_value)
-            vcat[1, part, :] = jnp.where(left, high.astype(F32), low.astype(F32)).astype(BF16)
-            vh0[1, part, :] = jnp.where(left, high.astype(F32), 0.0).astype(BF16)
-            squares = squares + jnp.sum(s_value * s_value, axis=0, keepdims=True)
-        csend[0, pl.ds(512, 8), :] = squares
-        pltpu.make_async_copy(solv, sol_hbm, out_sem.at[1]).start()
-
-        def panel(m, carry):
-            sp_copy(m).wait()
-            pend[...] = jnp.zeros_like(pend)
+            take_3(1, pend)
+
+        @pl.when(level > 3)
+        def _():
+            accp[...] = jnp.zeros_like(accp)
+
+        @pl.when(n_pan > 0)
+        def _():
+            sp_copy(jnp.int32(0)).wait()
+
+        for k in range(4):
+            packed = pl.ds(k * 128, 128)
+            size = 136 if k == 3 else 128
 
             @pl.when(level > 1)
             def _():
-                wait_child(0, m + 1, 512)
-                wait_child(1, m + 1, 512)
-                pend[...] = crecv[0, m + 1, 0:512, :] + crecv[1, m + 1, 0:512, :]
-
-            @pl.when(level == 3)
+                wait_child(0, 0, k, size)
+                accp[packed, :] = accp[packed, :] + crecv[0, 0, packed, :]
+
+            @pl.when((level > 1) & (level < 6))
             def _():
-                take_3(m + 1, pend)
-
-            slot = lax.rem(m, 3)
-
-            def body(i, inner):
-                high, low = split(spb[slot, rows(i * 256, 256), :])
-                product = dot(high, vcat[1]) + dot(low, vh0[1])
-                total = product + turned(product)
-                left = lane_left((128, 128))
-                part = rows(i * 128, 128)
-                csend[m, part, :] = jnp.where(left, total[:128], total[128:]) + pend[part, :]
-                return inner
-            lax.fori_loop(0, 4, body, 0)
-
-            @pl.when(m == 0)
+                wait_child(1, 0, k, size)
+                accp[packed, :] = accp[packed, :] + crecv[1, 0, packed, :]
+
+            left = lane_left((128, 128))
+            for j, value in enumerate(unpacked(accp[packed, :])):
+                part = pl.ds(k * 256 + j * 128, 128)
+                right_side = rhsp[part, :]
+                stacked(jnp.where(left, right_side, turned(right_side)) - value, 0, part)
+            part = pl.ds(k * 256, 256)
+            product = dot2(invb[part, k * 256:(k + 1) * 256], 0, part)
+            if k > 0:
+                product = product + racc[part, :]
+            s_value = product + turned(product)
+            stacked(s_value, 1, part)
+
+            @pl.when(n_pan > 0)
             def _():
-                up_copy(m, 520).start()
-
-            @pl.when(m > 0)
-            def _():
-                up_copy(m, 512).start()
-
-            @pl.when(m + 3 < n_pan)
-            def _():
-                sp_copy(m + 3).start()
-            return carry
-        lax.fori_loop(0, n_pan, panel, 0)
+                if k < 3:
+                    product = dot2(spb[0, :, k * 256:(k + 1) * 256], 1, part)
+                    cacc[...] = product if k == 0 else cacc[...] + product
+                else:
+                    squares[...] = squares[...] + jnp.sum(s_value * s_value, axis=0, keepdims=True)
+                    squares[...] = squares[...] + crecv_squares()
+                    csend[0, pl.ds(512, 8), :] = squares[...]
+                    for i in range(4):
+                        out = pl.ds(i * 256, 256)
+                        finished(cacc[out, :] + dot2(spb[0, out, k * 256:(k + 1) * 256], 1, part), 0, i)
+                        up_copy(0, i, 136 if i == 3 else 128).start()
+            solv[part, :] = s_value[:, :64]
+            if k < 3:
+                squares[...] = squares[...] + jnp.sum(s_value * s_value, axis=0, keepdims=True)
+                rest = slice((k + 1) * 256, 1024)
+                product = dot2(invb[rest, k * 256:(k + 1) * 256], 0, part)
+                racc[rest, :] = product if k == 0 else racc[rest, :] + product
+            else:
+                @pl.when(level == 6)
+                def _():
+                    squares[...] = squares[...] + jnp.sum(s_value * s_value, axis=0, keepdims=True) + crecv[0, 0, pl.ds(512, 8), :]
+
+        @pl.when(3 < n_pan)
+        def _():
+            sp_copy(jnp.int32(3)).start()
+        pltpu.make_async_copy(solv, sol_hbm, out_sem.at[1]).start()
+
+    def crecv_squares():
+        return jnp.where(level > 1, crecv[0, 0, pl.ds(512, 8), :] + crecv[1, 0, pl.ds(512, 8), :], 0.0)
+
+    def panel(m):
+        sp_copy(m).wait()
+
+        @pl.when(level == 3)
+        def _():
+            take_3(m + 1, pend)
+        slot = lax.rem(m, 3)
+        for i in range(4):
+            out = pl.ds(i * 256, 256)
+            finished(dot2(spb[slot, out, :], 1, slice(None)), m, i)
+            up_copy(m, i, 128).start()
+
+        @pl.when(m + 3 < n_pan)
+        def _():
+            sp_copy(m + 3).start()
 
     srhs_copy.wait()
-    rhsp[...] = jnp.zeros_like(rhsp)
     rhsp[:, :64] = rhsv[...]
     inv_copy.wait()
 
-    turn = jnp.minimum(level, 3) - 1
+    start_at = jnp.where(level == 1, 0, 5)
 
     def phase(p, carry):
-        @pl.when(p == turn)
-        def _():
-            chain()
-
-        @pl.when(p == 0)
-        def _():
-            gather_rs(2)
-            gather_rs(3)
-
-        @pl.when(p == 1)
-        def _():
-            gather_rs(4)
-            gather_rs(5)
+        @pl.when(p == start_at)
+        def _():
+            head()
+
+        @pl.when((p > 0) & (p < 5))
+        def _():
+            gather_rs(p + 1)
+
+        @pl.when((p > start_at) & (p - start_at < n_pan))
+        def _():
+            panel(p - start_at)
         return carry
-    lax.fori_loop(0, 3, phase, 0)
+    lax.fori_loop(0, 9, phase, 0)
 
     def width_copy(d):
         return pltpu.make_async_remote_copy(
@@ -448,7 +498,7 @@
 
     @pl.when(level == 6)
     def _():
-        wsend[0] = jnp.sqrt(csend[0, pl.ds(512, 8), :] / (32 * 3072) + 1e-06)
+        wsend[0] = jnp.sqrt(squares[...] / (32 * 3072) + 1e-06)
         for d in range(31):
             width_copy(d).start()
         width_ref[...] = wsend[0]
@@ -481,20 +531,21 @@
         wait_pieces(*piece_3(t))
 
     def sent(m, carry):
+        for i in range(3):
+            up_copy(m, i, 128).wait_send()
+
         @pl.when(m == 0)
         def _():
-            up_copy(m, 520).wait_send()
+            up_copy(m, 3, 136).wait_send()
 
         @pl.when(m > 0)
         def _():
-            up_copy(m, 512).wait_send()
+            up_copy(m, 3, 128).wait_send()
         return carry
     lax.fori_loop(0, n_pan, sent, 0)
 
 
 def local(rhs_rows, order, leaf_inverse, leaf_panels, panel_mask, sep_rhs, sep_inverse, sep_panels):
-    twice = jnp.broadcast_to(order.reshape(128, 1, 4), (128, 2, 4)).reshape(1024, 1)
-    mask = jnp.broadcast_to(panel_mask.reshape(24, 1).astype(BF16), (24, 128))
     vmem = pl.BlockSpec(memory_space=pltpu.VMEM)
     hbm = pl.BlockSpec(memory_space=pl.ANY)
     V = pltpu.VMEM
@@ -505,7 +556,7 @@
             jax.ShapeDtypeStruct((1024, 64), F32),
             jax.ShapeDtypeStruct((8, 128), F32),
         ),
-        in_specs=[vmem] * 3 + [hbm] * 5,
+        in_specs=[vmem, pl.BlockSpec(memory_space=pltpu.SMEM), vmem] + [hbm] * 5,
         out_specs=(hbm, hbm, vmem),
         scratch_shapes=[
             V((1024, 128), F32), V((1024, 128), F32),
@@ -518,7 +569,8 @@
             V((4, 3, 256, 128), F32),
             V((2, 2, 520, 128), F32), V((4, 2, 128, 128), F32),
             V((8192, 128), F32),
-            V((520, 128), F32), V((512, 128), F32),
+            V((512, 128), F32), V((512, 128), F32), V((8, 128), F32),
+            V((1024, 128), F32), V((1024, 128), F32),
             V((1024, 64), F32), V((1024, 128), F32),
             V((2, 1024, 128), BF16), V((2, 1024, 128), BF16),
             V((1024, 64), F32),
@@ -526,12 +578,12 @@
             V((5, 520, 128), F32), V((2, 5, 520, 128), F32),
             V((1, 8, 128), F32), V((1, 8, 128), F32),
             DMA((3,)), DMA((3,)), DMA((3,)), DMA((2,)), DMA((3,)), DMA((2,)), DMA, DMA((6,)), DMA((6,)),
-            DMA((4, 3)), DMA((4, 3)), DMA((2, 2)), DMA((4, 2)), DMA((4,)), DMA((5,)), DMA((2, 5)), DMA((2,)), DMA((2,)),
+            DMA((4, 3)), DMA((4, 3)), DMA((2, 2)), DMA((4, 2)), DMA((4,)), DMA((5, 4)), DMA((2, 5, 4)), DMA((2,)), DMA((2,)),
         ],
         compiler_params=pltpu.CompilerParams(
             collective_id=0, has_side_effects=True, vmem_limit_bytes=62 * 2 ** 20),
         cost_estimate=pl.CostEstimate(flops=7 * 10 ** 9, bytes_accessed=44 * 10 ** 6, transcendentals=0),
-    )(twice, mask, rhs_rows, leaf_inverse, leaf_panels[0], sep_rhs[0], sep_inverse[0], sep_panels[0])
+    )(order.reshape(4, 128), panel_mask[0], rhs_rows, leaf_inverse, leaf_panels[0], sep_rhs[0], sep_inverse[0], sep_panels[0])
     return leaf_y, solved[None], width[0, :64]
 
 

time: 224 us -> 199 us (0.89)
  Pallas kernels: 212 us -> 190 us
    pallas_call x1, Pallas kernels: 212 us -> 190 us  [local(): pl.pallas_call(kernel, out_shape=(jax.ShapeDtypeStruct((512, 256), F32),...]
where the time goes in v2:
time: 199 us
  Pallas kernels  190 us (95%)
  local copies, waits for them, and re-layouts  8.29 us (4%)
    pallas_call x1, Pallas kernels, local(): pl.pallas_call(kernel, out_shape=(jax.ShapeDtypeStruct((512, 256), F32),...  190 us
    unnamed x3, local copies, waits for them, and re-layouts  5.74 us

profile of v2, /device:TPU:16, one launch (start us, length us, event | category | flops | bytes accessed | tf_op | source)
XLA Modules:
  0.0 198.5 jit_solution(8847089221974720181)
XLA Ops:
  0.6 1.4 copy.12.mask_ref
  2.0 1.9 copy.11
  3.9 189.6 %shard_map.103 = (f32[512,256]{1,0:T(8,128)}, f32[1024,64]{1,0:T(8,128)}, f32[8,128]{1,0:T(8,128)}) custom-call(s32[4,128]{1,0:T(4,128)} %bitcast.14, s32[6,4]{1,0:T(8,128)} %copy.12.mask_ref, f32[512,256]{1,0:T(8,128)} %rhs_ref.1, f32[2048,512]{1,0:T(8,128)} %linv_hbm.1, f32[6,1024,512]{2,1,0:T(8,128)} %bitcast.10, f32[1024,64]{1,0:T(8,128)} %bitcast.12, ...), custom_call_target="tpu_custom_call" | custom-call | flops 7000000000 | bytes 44000000 | tf_op jit(solution)/shard_map/pallas_call | solution.py:552
  193.6 1.9 copy.13
  195.5 1.2 slice_bitcast_fusion
  196.7 1.9 copy.15

commit v3 on v2

--- a/solution.py
+++ b/solution.py
@@ -52,9 +52,9 @@
 def kernel(order_ref, mask_ref, rhs_ref, linv_hbm, lpan_hbm, srhs_hbm, sinv_hbm, span_hbm,
            leafy_hbm, sol_hbm, width_ref,
            abuf, xbuf, xh, xl, lbuf, zs, zr, za, ybuf, yh_s, yl_s, pbuf, own, snd, rcv, zrs,
-           pk12, pk3, ubuf, accp, pend, squares, cacc, racc, rhsv, rhsp, vcat, vh0, solv, invb, spb, csend, crecv, wsend, wrecv,
+           pk1, pk, zpair, yrs, s2, grecv, ubuf, accp, pend, squares, cacc, racc, rhsv, rhsp, vcat, vh0, solv, invb, spb, csend, crecv, wsend, wrecv,
            ld_sem, lp_sem, sp_sem, a2a_sem, zs_sem, zr_sem, za_sem, us_sem, ur_sem, rs_sem, rr_sem,
-           ps_sem, p3_sem, u_sem, cs_sem, cr_sem, w_sem, out_sem):
+           ps_sem, p3_sem, pair_sem, ys_sem, yr_sem, g_sem, u_sem, cs_sem, cr_sem, w_sem, out_sem):
     leaf = lax.axis_index("leaf")
     grid = lax.axis_index("grid")
     me = leaf * 4 + grid
@@ -62,6 +62,7 @@
     z = lax.rem(lax.div(leaf, 2), 4)
     x = lax.div(leaf, 8)
     yh = lax.div(grid, 2)
+    y = yh * 2 + yl
     c = lax.rem(grid, 2)
     sib = yh * 2 + 1 - c
 
@@ -73,6 +74,11 @@
         size = 2 ** (tier + 1)
         parent = jnp.where(level == tier, lax.div(leaf, size) * size + 2 ** tier - 1, parent)
     side = (leaf > parent).astype(jnp.int32)
+    above = jnp.int32(0)
+    for tier in range(1, 5):
+        size = 2 ** (tier + 2)
+        above = jnp.where(level == tier, lax.div(leaf, size) * size + 2 ** (tier + 1) - 1, above)
+    place = (parent > above).astype(jnp.int32) * 2 + side
     n_pan = 6 - level
 
     l_copy = pltpu.make_async_copy(linv_hbm, lbuf, ld_sem.at[0])
@@ -229,15 +235,21 @@
             def _():
                 pltpu.make_async_copy(src.at[to_yh], src.at[to_yh], sems.at[to_yh]).wait()
 
-    y_src = yl * 2 + yh
     leaf_1 = leaf - yl
     leaf_2 = (x * 4 + z - lax.rem(z, 2)) * 2 + 1
     leaf_3 = x * 8 + 3
-    piece_1 = (pk12.at[0], y_src * 520, 520, leaf_1, ps_sem.at[0])
-    piece_2 = (pk12.at[1, :, pl.ds(0, 512)], (lax.rem(z, 2) * 4 + y_src) * 512, 512, leaf_2, ps_sem.at[1])
+    half_z = lax.rem(z, 2)
+    piece_1 = (pk1, y * 520, 520, leaf_1, ps_sem)
+    piece_2 = (s2.at[0], half_z * 256 + y * 64, 64, leaf_2, p3_sem.at[0])
 
     def piece_3(t):
-        return (pk3.at[t - 2], ((t - 2) * 16 + y_src * 4 + z) * 128, 128, leaf_3, p3_sem.at[t - 2])
+        return (s2.at[t - 1, :, pl.ds(0, 32)], (t - 2) * 512 + z * 128 + y * 32, 32, leaf_3, p3_sem.at[t - 1])
+
+    def pair_copy():
+        return pltpu.make_async_remote_copy(
+            src_ref=own.at[1, rows((1 - half_z) * 512, 512)], dst_ref=zpair,
+            send_sem=pair_sem.at[0], recv_sem=pair_sem.at[1],
+            device_id=((x * 4 + z + 1 - 2 * half_z) * 2 + yl, grid), device_id_type=MESH)
 
     def rs_copy(t, k):
         at = z if t < 4 else x
@@ -248,31 +260,40 @@
             send_sem=rs_sem.at[t - 2, k - 1], recv_sem=rr_sem.at[t - 2, 3 - k],
             device_id=(to_leaf, grid), device_id_type=MESH)
 
+    def y_copy(t, k, size):
+        q = lax.rem(y + k, 4)
+        return pltpu.make_async_remote_copy(
+            src_ref=pk.at[t - 1, :, rows(q * size, size)], dst_ref=yrs.at[t - 1, 3 - k, :, pl.ds(0, size)],
+            send_sem=ys_sem.at[t - 1, k - 1], recv_sem=yr_sem.at[t - 1, 3 - k],
+            device_id=((x * 4 + z) * 2 + lax.rem(q, 2), lax.div(q, 2) * 2 + c), device_id_type=MESH)
+
     def spread(t):
         u_copy(t).wait_recv()
-        if t < 2:
+        if t == 0:
             def body(i, carry):
                 base = i * 256
                 top = own[t, rows(base, 128), :] + rcv[t, rows(base, 128), :]
                 bottom = own[t, rows(base + 128, 128), :] + rcv[t, rows(base + 128, 128), :]
                 p0, p1 = packed_pair(top, bottom)
-                pk12[t, 0, rows(i * 128, 128), :] = p0
-                pk12[t, 1, rows(i * 128, 128), :] = p1
+                pk1[0, rows(i * 128, 128), :] = p0
+                pk1[1, rows(i * 128, 128), :] = p1
                 return carry
             lax.fori_loop(0, 4, body, 0)
-            if t == 0:
-                squares = own[0, pl.ds(1024, 8), :] + rcv[0, pl.ds(1024, 8), :]
-                pk12[0, 0, pl.ds(512, 8), :] = squares
-                pk12[0, 1, pl.ds(512, 8), :] = turned(squares)
-            send_pieces(*(piece_1 if t == 0 else piece_2), u_sem.at[0])
+            squares = own[0, pl.ds(1024, 8), :] + rcv[0, pl.ds(1024, 8), :]
+            pk1[0, pl.ds(512, 8), :] = squares
+            pk1[1, pl.ds(512, 8), :] = turned(squares)
+            send_pieces(*piece_1, u_sem.at[0])
         else:
             def body(i, carry):
                 part = rows(i * 256, 256)
                 own[t, part, :] = own[t, part, :] + rcv[t, part, :]
                 return carry
             lax.fori_loop(0, 4, body, 0)
-            for k in range(1, 4):
-                rs_copy(t, k).start()
+            if t == 1:
+                pair_copy().start()
+            else:
+                for k in range(1, 4):
+                    rs_copy(t, k).start()
 
     for t in range(6):
         lp_copy(t).wait()
@@ -297,7 +318,22 @@
             spread(t - 1)
     spread(5)
 
-    def gather_rs(t):
+    def ring_start(t, size):
+        for k in range(1, 4):
+            y_copy(t, k, size).start()
+
+    def first_sum_2():
+        pair_copy().wait_recv()
+        for i in range(2):
+            base = half_z * 512 + i * 256
+            top = own[1, rows(base, 128), :] + zpair[pl.ds(i * 256, 128), :]
+            bottom = own[1, rows(base + 128, 128), :] + zpair[pl.ds(i * 256 + 128, 128), :]
+            p0, p1 = packed_pair(top, bottom)
+            pk[0, 0, pl.ds(i * 128, 128), :] = p0
+            pk[0, 1, pl.ds(i * 128, 128), :] = p1
+        ring_start(1, 64)
+
+    def first_sum(t):
         for k in range(3):
             pltpu.make_async_copy(zrs.at[t - 2, k], zrs.at[t - 2, k], rr_sem.at[t - 2, k]).wait()
         base = jnp.where(t < 4, z, x) * 256
@@ -308,9 +344,22 @@
                 value = value + zrs[t - 2, k, pl.ds(start, 128), :]
             return value
         p0, p1 = packed_pair(total(0), total(128))
-        pk3[t - 2, 0] = p0
-        pk3[t - 2, 1] = p1
-        send_pieces(*piece_3(t), u_sem.at[t - 2])
+        pk[t - 1, 0, pl.ds(0, 128), :] = p0
+        pk[t - 1, 1, pl.ds(0, 128), :] = p1
+        ring_start(t, 32)
+
+    def second_sum(t, size):
+        for k in range(3):
+            ref = yrs.at[t - 1, k, :, pl.ds(0, size)]
+            pltpu.make_async_copy(ref, ref, yr_sem.at[t - 1, k]).wait()
+        value = pk[t - 1, :, rows(y * size, size), :]
+        for k in range(3):
+            value = value + yrs[t - 1, k, :, pl.ds(0, size), :]
+        s2[t - 1, :, pl.ds(0, size), :] = value
+        if size == 64:
+            send_pieces(*piece_2, u_sem.at[0])
+        else:
+            send_pieces(*piece_3(t), u_sem.at[t - 2])
 
     def up_copy(m, i, size):
         part = rows(i * 128, size)
@@ -322,24 +371,39 @@
         part = rows(i * 128, size)
         pltpu.make_async_copy(csend.at[m, part], crecv.at[s, m, part], cr_sem.at[s, m, i]).wait()
 
+    def wait_whole(s, m):
+        ref = crecv.at[s, m, pl.ds(0, 512)]
+        pltpu.make_async_copy(ref, ref, cr_sem.at[s, m, 0]).wait()
+
     def take_3(k, dst):
-        start = k * 2048
-        pltpu.make_async_copy(ubuf.at[pl.ds(0, 1920)], ubuf.at[pl.ds(0, 1920)], u_sem.at[k]).wait()
+        start = k * 512
+        pltpu.make_async_copy(ubuf.at[pl.ds(0, 480)], ubuf.at[pl.ds(0, 480)], u_sem.at[k]).wait()
 
         @pl.when(k < 2)
         def _():
-            value = ubuf[rows(start, 512), :]
+            dst[...] = ubuf[rows(start, 512), :]
+
+        @pl.when(k >= 2)
+        def _():
+            value = ubuf[rows(start, 128), :]
             for s in range(1, 4):
-                value = value + ubuf[rows(start + s * 512, 512), :]
-            dst[...] = value
-
-        @pl.when(k >= 2)
-        def _():
-            value = ubuf[rows(start, 128), :]
-            for s in range(1, 16):
                 value = value + ubuf[rows(start + s * 128, 128), :]
             dst[...] = jnp.zeros_like(dst)
             dst[rows(x * 128, 128), :] = value
+
+    def far_copy():
+        return pltpu.make_async_remote_copy(
+            src_ref=csend.at[1, pl.ds(0, 512)], dst_ref=grecv.at[place],
+            send_sem=cs_sem.at[1, 0], recv_sem=g_sem.at[place], device_id=(above, grid), device_id_type=MESH)
+
+    def whole_copy(m):
+        return pltpu.make_async_remote_copy(
+            src_ref=csend.at[m, pl.ds(0, 512)], dst_ref=crecv.at[side, m, pl.ds(0, 512)],
+            send_sem=cs_sem.at[m, 0], recv_sem=cr_sem.at[side, m, 0], device_id=(parent, grid), device_id_type=MESH)
+
+    def take_far(slot):
+        pltpu.make_async_copy(grecv.at[slot], grecv.at[slot], g_sem.at[slot]).wait()
+        accp[...] = accp[...] + grecv[slot]
 
     def dot2(a, which, part):
         high, low = split(a)
@@ -360,12 +424,6 @@
         def _():
             csend[m, part, :] = csend[m, part, :] + pend[part, :]
 
-        @pl.when(level > 1)
-        def _():
-            wait_child(0, m + 1, i, 128)
-            wait_child(1, m + 1, i, 128)
-            csend[m, part, :] = csend[m, part, :] + (crecv[0, m + 1, part, :] + crecv[1, m + 1, part, :])
-
     def head():
         squares[...] = jnp.zeros_like(squares)
 
@@ -377,11 +435,8 @@
 
         @pl.when(level == 2)
         def _():
-            pltpu.make_async_copy(ubuf.at[pl.ds(0, 3584)], ubuf.at[pl.ds(0, 3584)], u_sem.at[0]).wait()
-            value = ubuf[0:512, :]
-            for s in range(1, 8):
-                value = value + ubuf[s * 512:(s + 1) * 512, :]
-            accp[...] = value
+            pltpu.make_async_copy(ubuf.at[pl.ds(0, 448)], ubuf.at[pl.ds(0, 448)], u_sem.at[0]).wait()
+            accp[...] = ubuf[0:512, :]
 
         @pl.when(level == 3)
         def _():
@@ -391,6 +446,16 @@
         @pl.when(level > 3)
         def _():
             accp[...] = jnp.zeros_like(accp)
+
+        @pl.when(level > 2)
+        def _():
+            take_far(0)
+            take_far(1)
+
+        @pl.when((level > 2) & (level < 6))
+        def _():
+            take_far(2)
+            take_far(3)
 
         @pl.when(n_pan > 0)
         def _():
@@ -464,7 +529,21 @@
         for i in range(4):
             out = pl.ds(i * 256, 256)
             finished(dot2(spb[slot, out, :], 1, slice(None)), m, i)
-            up_copy(m, i, 128).start()
+
+        @pl.when(level > 1)
+        def _():
+            for s in range(2):
+                wait_whole(s, m + 1)
+            csend[m, pl.ds(0, 512), :] = csend[m, pl.ds(0, 512), :] + (
+                crecv[0, m + 1, pl.ds(0, 512), :] + crecv[1, m + 1, pl.ds(0, 512), :])
+
+        @pl.when(m == 1)
+        def _():
+            far_copy().start()
+
+        @pl.when(m > 1)
+        def _():
+            whole_copy(m).start()
 
         @pl.when(m + 3 < n_pan)
         def _():
@@ -477,13 +556,25 @@
     start_at = jnp.where(level == 1, 0, 5)
 
     def phase(p, carry):
+        @pl.when(p == 0)
+        def _():
+            first_sum_2()
+
+        @pl.when((p > 0) & (p < 5))
+        def _():
+            first_sum(p + 1)
+
+        @pl.when(p == 1)
+        def _():
+            second_sum(1, 64)
+
+        @pl.when((p > 1) & (p < 6))
+        def _():
+            second_sum(p, 32)
+
         @pl.when(p == start_at)
         def _():
             head()
-
-        @pl.when((p > 0) & (p < 5))
-        def _():
-            gather_rs(p + 1)
 
         @pl.when((p > start_at) & (p - start_at < n_pan))
         def _():
@@ -524,23 +615,29 @@
     for t in range(6):
         u_copy(t).wait_send()
     wait_pieces(*piece_1)
+    pair_copy().wait_send()
+    for k in range(1, 4):
+        y_copy(1, k, 64).wait_send()
     wait_pieces(*piece_2)
     for t in range(2, 6):
         for k in range(1, 4):
             rs_copy(t, k).wait_send()
+            y_copy(t, k, 32).wait_send()
         wait_pieces(*piece_3(t))
 
     def sent(m, carry):
-        for i in range(3):
-            up_copy(m, i, 128).wait_send()
-
         @pl.when(m == 0)
         def _():
-            up_copy(m, 3, 136).wait_send()
-
-        @pl.when(m > 0)
-        def _():
-            up_copy(m, 3, 128).wait_send()
+            for i in range(4):
+                up_copy(0, i, 136 if i == 3 else 128).wait_send()
+
+        @pl.when(m == 1)
+        def _():
+            far_copy().wait_send()
+
+        @pl.when(m > 1)
+        def _():
+            whole_copy(m).wait_send()
         return carry
     lax.fori_loop(0, n_pan, sent, 0)
 
@@ -567,8 +664,10 @@
             V((3, 1024, 512), F32),
             V((6, 1032, 128), F32), V((6, 1032, 128), F32), V((6, 1032, 128), F32),
             V((4, 3, 256, 128), F32),
-            V((2, 2, 520, 128), F32), V((4, 2, 128, 128), F32),
-            V((8192, 128), F32),
+            V((2, 520, 128), F32), V((5, 2, 256, 128), F32),
+            V((512, 128), F32), V((5, 3, 2, 64, 128), F32),
+            V((5, 2, 64, 128), F32), V((4, 512, 128), F32),
+            V((2080, 128), F32),
             V((512, 128), F32), V((512, 128), F32), V((8, 128), F32),
             V((1024, 128), F32), V((1024, 128), F32),
             V((1024, 64), F32), V((1024, 128), F32),
@@ -578,7 +677,8 @@
             V((5, 520, 128), F32), V((2, 5, 520, 128), F32),
             V((1, 8, 128), F32), V((1, 8, 128), F32),
             DMA((3,)), DMA((3,)), DMA((3,)), DMA((2,)), DMA((3,)), DMA((2,)), DMA, DMA((6,)), DMA((6,)),
-            DMA((4, 3)), DMA((4, 3)), DMA((2, 2)), DMA((4, 2)), DMA((4,)), DMA((5, 4)), DMA((2, 5, 4)), DMA((2,)), DMA((2,)),
+            DMA((4, 3)), DMA((4, 3)),
+            DMA((2,)), DMA((5, 2)), DMA((2,)), DMA((5, 3)), DMA((5, 3)), DMA((4,)), DMA((4,)), DMA((5, 4)), DMA((2, 5, 4)), DMA((2,)), DMA((2,)),
         ],
         compiler_params=pltpu.CompilerParams(
             collective_id=0, has_side_effects=True, vmem_limit_bytes=62 * 2 ** 20),

time: 199 us -> 175 us (0.88)
  Pallas kernels: 190 us -> 164 us
    pallas_call x1, Pallas kernels: 190 us -> 164 us  [local(): pl.pallas_call(kernel, out_shape=(jax.ShapeDtypeStruct((512, 256), F32),...]
where the time goes in v3:
time: 175 us; the launch traced here: 173 us
  Pallas kernels  164 us (94%)
  local copies, waits for them, and re-layouts  8.29 us (5%)
    pallas_call x1, Pallas kernels, local(): pl.pallas_call(kernel, out_shape=(jax.ShapeDtypeStruct((512, 256), F32),...  164 us
    unnamed x3, local copies, waits for them, and re-layouts  5.74 us

profile of v3, /device:TPU:16, one launch (start us, length us, event | category | flops | bytes accessed | tf_op | source)
XLA Modules:
  0.0 173.1 jit_solution(1584899282623104619)
XLA Ops:
  0.6 1.4 copy.12.mask_ref
  2.0 1.9 %copy.11 = f32[1,1024,64]{2,1,0:T(8,128)} copy(f32[1,1024,64]{1,2,0:T(8,128)} %param.13) | data formatting | bytes 524288 | tf_op args[5]
  3.9 164.2 %shard_map.103 = (f32[512,256]{1,0:T(8,128)}, f32[1024,64]{1,0:T(8,128)}, f32[8,128]{1,0:T(8,128)}) custom-call(s32[4,128]{1,0:T(4,128)} %bitcast.14, s32[6,4]{1,0:T(8,128)} %copy.12.mask_ref, f32[512,256]{1,0:T(8,128)} %rhs_ref.1, f32[2048,512]{1,0:T(8,128)} %linv_hbm.1, f32[6,1024,512]{2,1,0:T(8,128)} %bitcast.10, f32[1024,64]{1,0:T(8,128)} %bitcast.12, ...), custom_call_target="tpu_custom_call" | custom-call | flops 7000000000 | bytes 44000000 | tf_op jit(solution)/shard_map/pallas_call | solution.py:649
  168.1 1.9 %copy.13 = f32[1,1024,64]{1,2,0:T(8,128)} copy(f32[1,1024,64]{2,1,0:T(8,128)} %bitcast.13) | data formatting | bytes 524288
  170.0 1.2 slice_bitcast_fusion
  171.2 1.9 %copy.15 = f32[512,256]{1,0:T(8,128)} copy(f32[512,256]{1,0:T(8,128)} %get-tuple-element.15) | data formatting | bytes 1048576

commit v4 on v3

--- a/solution.py
+++ b/solution.py
@@ -52,9 +52,9 @@
 def kernel(order_ref, mask_ref, rhs_ref, linv_hbm, lpan_hbm, srhs_hbm, sinv_hbm, span_hbm,
            leafy_hbm, sol_hbm, width_ref,
            abuf, xbuf, xh, xl, lbuf, zs, zr, za, ybuf, yh_s, yl_s, pbuf, own, snd, rcv, zrs,
-           pk1, pk, zpair, yrs, s2, grecv, ubuf, accp, pend, squares, cacc, racc, rhsv, rhsp, vcat, vh0, solv, invb, spb, csend, crecv, wsend, wrecv,
+           pk1, pk, zpair, yrs, s2, grecv, ubuf, accp, pend, squares, cacc, racc, rhsv, rhsp, vcat, vh0, solv, invb, spb, csend, crecv, relay, xrs, qsend, qrecv, top, wsend, wrecv,
            ld_sem, lp_sem, sp_sem, a2a_sem, zs_sem, zr_sem, za_sem, us_sem, ur_sem, rs_sem, rr_sem,
-           ps_sem, p3_sem, pair_sem, ys_sem, yr_sem, g_sem, u_sem, cs_sem, cr_sem, w_sem, out_sem):
+           relay_sem, xr_sem, q_sem, qr_sem, top_sem, ps_sem, p3_sem, pair_sem, ys_sem, yr_sem, g_sem, u_sem, cs_sem, cr_sem, w_sem, out_sem):
     leaf = lax.axis_index("leaf")
     grid = lax.axis_index("grid")
     me = leaf * 4 + grid
@@ -297,7 +297,7 @@
 
     for t in range(6):
         lp_copy(t).wait()
-        masks = [jnp.full((1, 256), mask_ref[t, b].astype(F32)).astype(BF16) for b in range(4)]
+        masks = [jnp.full((1, 256), mask_ref[b, t].astype(F32)).astype(BF16) for b in range(4)]
         masked = lambda ref: jnp.concatenate(
             [ref[b * 128:(b + 1) * 128, :] * masks[b] for b in range(4)], axis=0)
         y_high, y_low = masked(yh_s), masked(yl_s)
@@ -361,45 +361,72 @@
         else:
             send_pieces(*piece_3(t), u_sem.at[t - 2])
 
-    def up_copy(m, i, size):
+    def up_copy(i, size):
         part = rows(i * 128, size)
         return pltpu.make_async_remote_copy(
-            src_ref=csend.at[m, part], dst_ref=crecv.at[side, m, part],
-            send_sem=cs_sem.at[m, i], recv_sem=cr_sem.at[side, m, i], device_id=(parent, grid), device_id_type=MESH)
-
-    def wait_child(s, m, i, size):
+            src_ref=csend.at[0, part], dst_ref=crecv.at[side, part],
+            send_sem=cs_sem.at[0, i], recv_sem=cr_sem.at[side, i], device_id=(parent, grid), device_id_type=MESH)
+
+    def wait_child(s, i, size):
         part = rows(i * 128, size)
-        pltpu.make_async_copy(csend.at[m, part], crecv.at[s, m, part], cr_sem.at[s, m, i]).wait()
-
-    def wait_whole(s, m):
-        ref = crecv.at[s, m, pl.ds(0, 512)]
-        pltpu.make_async_copy(ref, ref, cr_sem.at[s, m, 0]).wait()
-
-    def take_3(k, dst):
-        start = k * 512
-        pltpu.make_async_copy(ubuf.at[pl.ds(0, 480)], ubuf.at[pl.ds(0, 480)], u_sem.at[k]).wait()
-
-        @pl.when(k < 2)
-        def _():
-            dst[...] = ubuf[rows(start, 512), :]
-
-        @pl.when(k >= 2)
-        def _():
-            value = ubuf[rows(start, 128), :]
-            for s in range(1, 4):
-                value = value + ubuf[rows(start + s * 128, 128), :]
-            dst[...] = jnp.zeros_like(dst)
-            dst[rows(x * 128, 128), :] = value
+        pltpu.make_async_copy(csend.at[0, part], crecv.at[s, part], cr_sem.at[s, i]).wait()
 
     def far_copy():
         return pltpu.make_async_remote_copy(
             src_ref=csend.at[1, pl.ds(0, 512)], dst_ref=grecv.at[place],
             send_sem=cs_sem.at[1, 0], recv_sem=g_sem.at[place], device_id=(above, grid), device_id_type=MESH)
 
-    def whole_copy(m):
-        return pltpu.make_async_remote_copy(
-            src_ref=csend.at[m, pl.ds(0, 512)], dst_ref=crecv.at[side, m, pl.ds(0, 512)],
-            send_sem=cs_sem.at[m, 0], recv_sem=cr_sem.at[side, m, 0], device_id=(parent, grid), device_id_type=MESH)
+    def relay_copy():
+        return pltpu.make_async_remote_copy(
+            src_ref=csend.at[2, pl.ds(0, 512)], dst_ref=relay.at[side],
+            send_sem=cs_sem.at[2, 0], recv_sem=relay_sem.at[side], device_id=(parent, grid), device_id_type=MESH)
+
+    def x_copy(m, u, k):
+        q = lax.rem(x + k, 4)
+        return pltpu.make_async_remote_copy(
+            src_ref=csend.at[m, rows(q * 128, 128)], dst_ref=xrs.at[u, 3 - k],
+            send_sem=cs_sem.at[m, k], recv_sem=xr_sem.at[u, 3 - k],
+            device_id=((q * 4 + z) * 2 + yl, grid), device_id_type=MESH)
+
+    def quarter_copy(u):
+        return pltpu.make_async_remote_copy(
+            src_ref=qsend.at[u], dst_ref=qrecv.at[u, side],
+            send_sem=q_sem.at[u], recv_sem=qr_sem.at[u, side], device_id=(parent, grid), device_id_type=MESH)
+
+    def top_copy(u):
+        return pltpu.make_async_remote_copy(
+            src_ref=qsend.at[u], dst_ref=top.at[rows(x * 128, 128)],
+            send_sem=q_sem.at[u], recv_sem=top_sem, device_id=(15 + 16 * u, grid), device_id_type=MESH)
+
+    def x_sum(u):
+        for k in range(3):
+            pltpu.make_async_copy(xrs.at[u, k], xrs.at[u, k], xr_sem.at[u, k]).wait()
+        m = 4 - level + u
+        qsend[u] = csend[m, rows(x * 128, 128), :] + xrs[u, 0] + (xrs[u, 1] + xrs[u, 2])
+
+        @pl.when(level > 1)
+        def _():
+            for s in range(2):
+                pltpu.make_async_copy(qrecv.at[u, s], qrecv.at[u, s], qr_sem.at[u, s]).wait()
+            qsend[u] = qsend[u] + (qrecv[u, 0] + qrecv[u, 1])
+
+        @pl.when(level < 3)
+        def _():
+            quarter_copy(u).start()
+
+        @pl.when(level == 3)
+        def _():
+            pltpu.make_async_copy(ubuf.at[pl.ds(0, 480)], ubuf.at[pl.ds(0, 480)], u_sem.at[2 + u]).wait()
+            start = (2 + u) * 512
+            value = qsend[u]
+            for s in range(4):
+                value = value + ubuf[rows(start + s * 128, 128), :]
+            qsend[u] = value
+            top_copy(u).start()
+
+    def take_3(k, dst):
+        pltpu.make_async_copy(ubuf.at[pl.ds(0, 480)], ubuf.at[pl.ds(0, 480)], u_sem.at[k]).wait()
+        dst[...] = ubuf[k * 512:(k + 1) * 512, :]
 
     def take_far(slot):
         pltpu.make_async_copy(grecv.at[slot], grecv.at[slot], g_sem.at[slot]).wait()
@@ -420,10 +447,6 @@
         part = rows(i * 128, 128)
         csend[m, part, :] = jnp.where(lane_left((128, 128)), total[:128], total[128:])
 
-        @pl.when(level == 3)
-        def _():
-            csend[m, part, :] = csend[m, part, :] + pend[part, :]
-
     def head():
         squares[...] = jnp.zeros_like(squares)
 
@@ -447,15 +470,20 @@
         def _():
             accp[...] = jnp.zeros_like(accp)
 
-        @pl.when(level > 2)
+        @pl.when((level > 2) & (level != 5))
         def _():
             take_far(0)
             take_far(1)
 
-        @pl.when((level > 2) & (level < 6))
+        @pl.when((level == 3) | (level == 4))
         def _():
             take_far(2)
             take_far(3)
+
+        @pl.when(level > 4)
+        def _():
+            pltpu.make_async_copy(top, top, top_sem).wait()
+            accp[...] = accp[...] + top[...]
 
         @pl.when(n_pan > 0)
         def _():
@@ -467,13 +495,13 @@
 
             @pl.when(level > 1)
             def _():
-                wait_child(0, 0, k, size)
-                accp[packed, :] = accp[packed, :] + crecv[0, 0, packed, :]
+                wait_child(0, k, size)
+                accp[packed, :] = accp[packed, :] + crecv[0, packed, :]
 
             @pl.when((level > 1) & (level < 6))
             def _():
-                wait_child(1, 0, k, size)
-                accp[packed, :] = accp[packed, :] + crecv[1, 0, packed, :]
+                wait_child(1, k, size)
+                accp[packed, :] = accp[packed, :] + crecv[1, packed, :]
 
             left = lane_left((128, 128))
             for j, value in enumerate(unpacked(accp[packed, :])):
@@ -499,8 +527,13 @@
                     for i in range(4):
                         out = pl.ds(i * 256, 256)
                         finished(cacc[out, :] + dot2(spb[0, out, k * 256:(k + 1) * 256], 1, part), 0, i)
-                        up_copy(0, i, 136 if i == 3 else 128).start()
-            solv[part, :] = s_value[:, :64]
+
+                        @pl.when(level == 3)
+                        def _():
+                            up = pl.ds(i * 128, 128)
+                            csend[0, up, :] = csend[0, up, :] + pend[up, :]
+                        up_copy(i, 136 if i == 3 else 128).start()
+            solv[:, k * 256:(k + 1) * 256] = jnp.transpose(s_value)[:64]
             if k < 3:
                 squares[...] = squares[...] + jnp.sum(s_value * s_value, axis=0, keepdims=True)
                 rest = slice((k + 1) * 256, 1024)
@@ -509,7 +542,7 @@
             else:
                 @pl.when(level == 6)
                 def _():
-                    squares[...] = squares[...] + jnp.sum(s_value * s_value, axis=0, keepdims=True) + crecv[0, 0, pl.ds(512, 8), :]
+                    squares[...] = squares[...] + jnp.sum(s_value * s_value, axis=0, keepdims=True) + crecv[0, pl.ds(512, 8), :]
 
         @pl.when(3 < n_pan)
         def _():
@@ -517,43 +550,45 @@
         pltpu.make_async_copy(solv, sol_hbm, out_sem.at[1]).start()
 
     def crecv_squares():
-        return jnp.where(level > 1, crecv[0, 0, pl.ds(512, 8), :] + crecv[1, 0, pl.ds(512, 8), :], 0.0)
+        return jnp.where(level > 1, crecv[0, pl.ds(512, 8), :] + crecv[1, pl.ds(512, 8), :], 0.0)
 
     def panel(m):
         sp_copy(m).wait()
-
-        @pl.when(level == 3)
-        def _():
-            take_3(m + 1, pend)
         slot = lax.rem(m, 3)
         for i in range(4):
             out = pl.ds(i * 256, 256)
             finished(dot2(spb[slot, out, :], 1, slice(None)), m, i)
-
-        @pl.when(level > 1)
+        over_x = (level < 4) & (m >= 4 - level)
+
+        @pl.when((level == 2) & (m == 1))
         def _():
             for s in range(2):
-                wait_whole(s, m + 1)
-            csend[m, pl.ds(0, 512), :] = csend[m, pl.ds(0, 512), :] + (
-                crecv[0, m + 1, pl.ds(0, 512), :] + crecv[1, m + 1, pl.ds(0, 512), :])
-
-        @pl.when(m == 1)
+                pltpu.make_async_copy(relay.at[s], relay.at[s], relay_sem.at[s]).wait()
+            csend[1, pl.ds(0, 512), :] = csend[1, pl.ds(0, 512), :] + (relay[0] + relay[1])
+
+        @pl.when((m == 1) & jnp.logical_not(over_x))
         def _():
             far_copy().start()
 
-        @pl.when(m > 1)
-        def _():
-            whole_copy(m).start()
+        @pl.when((level == 1) & (m == 2))
+        def _():
+            relay_copy().start()
+
+        @pl.when(over_x)
+        def _():
+            for k in range(1, 4):
+                x_copy(m, m - 4 + level, k).start()
 
         @pl.when(m + 3 < n_pan)
         def _():
             sp_copy(m + 3).start()
 
     srhs_copy.wait()
-    rhsp[:, :64] = rhsv[...]
+    for k in range(4):
+        rhsp[k * 256:(k + 1) * 256, :64] = jnp.transpose(rhsv[:, k * 256:(k + 1) * 256])
     inv_copy.wait()
 
-    start_at = jnp.where(level == 1, 0, 5)
+    start_at = jnp.minimum(2 * (level - 1), 5)
 
     def phase(p, carry):
         @pl.when(p == 0)
@@ -576,11 +611,17 @@
         def _():
             head()
 
-        @pl.when((p > start_at) & (p - start_at < n_pan))
-        def _():
-            panel(p - start_at)
+        m = p - start_at
+
+        @pl.when((m > 0) & (m < n_pan))
+        def _():
+            panel(m)
+
+        @pl.when((level < 4) & ((m == 5 - level) | (m == 6 - level)))
+        def _():
+            x_sum(m - 5 + level)
         return carry
-    lax.fori_loop(0, 9, phase, 0)
+    lax.fori_loop(0, 8, phase, 0)
 
     def width_copy(d):
         return pltpu.make_async_remote_copy(
@@ -625,21 +666,35 @@
             y_copy(t, k, 32).wait_send()
         wait_pieces(*piece_3(t))
 
-    def sent(m, carry):
-        @pl.when(m == 0)
-        def _():
-            for i in range(4):
-                up_copy(0, i, 136 if i == 3 else 128).wait_send()
-
-        @pl.when(m == 1)
-        def _():
-            far_copy().wait_send()
-
-        @pl.when(m > 1)
-        def _():
-            whole_copy(m).wait_send()
-        return carry
-    lax.fori_loop(0, n_pan, sent, 0)
+    @pl.when(n_pan > 0)
+    def _():
+        for i in range(4):
+            up_copy(i, 136 if i == 3 else 128).wait_send()
+
+    @pl.when((level < 3) | (level == 4))
+    def _():
+        far_copy().wait_send()
+
+    @pl.when(level == 1)
+    def _():
+        relay_copy().wait_send()
+
+    @pl.when(level < 4)
+    def _():
+        for u in range(2):
+            for k in range(1, 4):
+                x_copy(4 - level + u, u, k).wait_send()
+            quarter_copy(u).wait_send()
+
+
+def write_out(y_in, s_in, w_in, y_out, s_out, w_out, sem):
+    first = pltpu.make_async_copy(y_in, y_out, sem.at[0])
+    second = pltpu.make_async_copy(s_in, s_out, sem.at[1])
+    first.start()
+    second.start()
+    w_out[...] = w_in[0, :64]
+    first.wait()
+    second.wait()
 
 
 def local(rhs_rows, order, leaf_inverse, leaf_panels, panel_mask, sep_rhs, sep_inverse, sep_panels):
@@ -650,7 +705,7 @@
         kernel,
         out_shape=(
             jax.ShapeDtypeStruct((512, 256), F32),
-            jax.ShapeDtypeStruct((1024, 64), F32),
+            jax.ShapeDtypeStruct((64, 1024), F32),
             jax.ShapeDtypeStruct((8, 128), F32),
         ),
         in_specs=[vmem, pl.BlockSpec(memory_space=pltpu.SMEM), vmem] + [hbm] * 5,
@@ -670,21 +725,34 @@
             V((2080, 128), F32),
             V((512, 128), F32), V((512, 128), F32), V((8, 128), F32),
             V((1024, 128), F32), V((1024, 128), F32),
-            V((1024, 64), F32), V((1024, 128), F32),
+            V((64, 1024), F32), V((1024, 128), F32),
             V((2, 1024, 128), BF16), V((2, 1024, 128), BF16),
-            V((1024, 64), F32),
+            V((64, 1024), F32),
             V((1024, 1024), F32), V((3, 1024, 1024), F32),
-            V((5, 520, 128), F32), V((2, 5, 520, 128), F32),
+            V((5, 520, 128), F32), V((2, 520, 128), F32), V((2, 512, 128), F32),
+            V((2, 3, 128, 128), F32), V((2, 128, 128), F32), V((2, 2, 128, 128), F32), V((512, 128), F32),
             V((1, 8, 128), F32), V((1, 8, 128), F32),
             DMA((3,)), DMA((3,)), DMA((3,)), DMA((2,)), DMA((3,)), DMA((2,)), DMA, DMA((6,)), DMA((6,)),
             DMA((4, 3)), DMA((4, 3)),
-            DMA((2,)), DMA((5, 2)), DMA((2,)), DMA((5, 3)), DMA((5, 3)), DMA((4,)), DMA((4,)), DMA((5, 4)), DMA((2, 5, 4)), DMA((2,)), DMA((2,)),
+            DMA((2,)), DMA((2, 3)), DMA((2,)), DMA((2, 2)), DMA,
+            DMA((2,)), DMA((5, 2)), DMA((2,)), DMA((5, 3)), DMA((5, 3)), DMA((4,)), DMA((4,)), DMA((5, 4)), DMA((2, 4)), DMA((2,)), DMA((2,)),
         ],
         compiler_params=pltpu.CompilerParams(
             collective_id=0, has_side_effects=True, vmem_limit_bytes=62 * 2 ** 20),
         cost_estimate=pl.CostEstimate(flops=7 * 10 ** 9, bytes_accessed=44 * 10 ** 6, transcendentals=0),
-    )(order.reshape(4, 128), panel_mask[0], rhs_rows, leaf_inverse, leaf_panels[0], sep_rhs[0], sep_inverse[0], sep_panels[0])
-    return leaf_y, solved[None], width[0, :64]
+    )(order.reshape(4, 128), panel_mask[0].T, rhs_rows, leaf_inverse, leaf_panels[0], sep_rhs[0].T, sep_inverse[0], sep_panels[0])
+    leaf_y, solved, width = pl.pallas_call(
+        write_out,
+        out_shape=(
+            jax.ShapeDtypeStruct((512, 256), F32),
+            jax.ShapeDtypeStruct((64, 1024), F32),
+            jax.ShapeDtypeStruct((64,), F32),
+        ),
+        in_specs=[hbm, hbm, vmem],
+        out_specs=(hbm, hbm, vmem),
+        scratch_shapes=[DMA((2,))],
+    )(leaf_y, solved, width)
+    return leaf_y, solved.T[None], width
 
 
 def solution(mesh):

time: 175 us -> 175 us (level)
  Pallas kernels: 164 us -> 174 us
  local copies, waits for them, and re-layouts: 8.29 us -> 0 us
    pallas_call x0 -> x1, Pallas kernels: none -> 26.1 us  [local(): pl.pallas_call(write_out, out_shape=(jax.ShapeDtypeStruct((512, 256), F32...]
    pallas_call x1, Pallas kernels: 164 us -> 148 us  [local(): pl.pallas_call(kernel, out_shape=(jax.ShapeDtypeStruct((512, 256), F32),...]
    unnamed x3 -> x0, local copies, waits for them, and re-layouts: 5.74 us -> none
    squeeze x2 -> x0, local copies, waits for them, and re-layouts: 2.54 us -> none  [the longest x1 1.35 us: local(): panel_mask[0]]
where the time goes in v4:
time: 175 us; the launch traced here: 174 us
  Pallas kernels  174 us (99%)
    pallas_call x1, Pallas kernels, local(): pl.pallas_call(kernel, out_shape=(jax.ShapeDtypeStruct((512, 256), F32),...  148 us
    pallas_call x1, Pallas kernels, local(): pl.pallas_call(write_out, out_shape=(jax.ShapeDtypeStruct((512, 256), F32...  26.1 us

profile of v4, /device:TPU:16, one launch (start us, length us, event | category | flops | bytes accessed | tf_op | source)
XLA Modules:
  0.0 174.4 jit_solution(9318096275217288126)
XLA Ops:
  0.6 147.7 %shard_map.103 = (f32[512,256]{1,0:T(8,128)}, f32[64,1024]{1,0:T(8,128)}, f32[8,128]{1,0:T(8,128)}) custom-call(s32[4,128]{1,0:T(4,128)} %bitcast.17, s32[4,6]{1,0:T(4,128)} %bitcast.18, f32[512,256]{1,0:T(8,128)} %rhs_ref.1, f32[2048,512]{1,0:T(8,128)} %linv_hbm.1, f32[6,1024,512]{2,1,0:T(8,128)} %bitcast.14, f32[64,1024]{1,0:T(8,128)} %bitcast.16, ...), custom_call_target="tpu_custom_call" | custom-call | flops 7000000000 | bytes 44000000 | tf_op jit(solution)/shard_map/pallas_call | solution.py:704
  148.3 26.1 %shard_map.104 = (f32[512,256]{1,0:T(8,128)}, f32[64,1024]{1,0:T(8,128)}, f32[64]{0:T(128)}) custom-call(f32[512,256]{1,0:T(8,128)} %get-tuple-element.9.y_in, f32[64,1024]{1,0:T(8,128)} %get-tuple-element.10.s_in, f32[8,128]{1,0:T(8,128)} %get-tuple-element.11.w_in), custom_call_target="tpu_custom_call" | custom-call | tf_op jit(solution)/shard_map/pallas_call | solution.py:744

commit v5 on v4

--- a/solution.py
+++ b/solution.py
@@ -687,14 +687,10 @@
             quarter_copy(u).wait_send()
 
 
-def write_out(y_in, s_in, w_in, y_out, s_out, w_out, sem):
-    first = pltpu.make_async_copy(y_in, y_out, sem.at[0])
-    second = pltpu.make_async_copy(s_in, s_out, sem.at[1])
-    first.start()
-    second.start()
+def write_out(y_in, s_in, w_in, y_out, s_out, w_out):
+    y_out[...] = y_in[...]
+    s_out[...] = s_in[...]
     w_out[...] = w_in[0, :64]
-    first.wait()
-    second.wait()
 
 
 def local(rhs_rows, order, leaf_inverse, leaf_panels, panel_mask, sep_rhs, sep_inverse, sep_panels):
@@ -748,9 +744,8 @@
             jax.ShapeDtypeStruct((64, 1024), F32),
             jax.ShapeDtypeStruct((64,), F32),
         ),
-        in_specs=[hbm, hbm, vmem],
-        out_specs=(hbm, hbm, vmem),
-        scratch_shapes=[DMA((2,))],
+        in_specs=[vmem] * 3,
+        out_specs=(vmem,) * 3,
     )(leaf_y, solved, width)
     return leaf_y, solved.T[None], width
 

time: 175 us -> 151 us (0.86)
  Pallas kernels: 174 us -> 150 us
    pallas_call x1, Pallas kernels: 26.1 us -> 2.03 us  [local(): pl.pallas_call(write_out, out_shape=(jax.ShapeDtypeStruct((512, 256), F32...]
where the time goes in v5:
time: 151 us; the launch traced here: 150 us
  Pallas kernels  150 us (99%)
    pallas_call x1, Pallas kernels, local(): pl.pallas_call(kernel, out_shape=(jax.ShapeDtypeStruct((512, 256), F32),...  148 us

profile of v5, /device:TPU:16, one launch (start us, length us, event | category | flops | bytes accessed | tf_op | source)
XLA Modules:
  0.0 150.4 jit_solution(1881988328376308520)
XLA Ops:
  0.6 147.7 %shard_map.103 = (f32[512,256]{1,0:T(8,128)}, f32[64,1024]{1,0:T(8,128)}, f32[8,128]{1,0:T(8,128)}) custom-call(s32[4,128]{1,0:T(4,128)} %bitcast.17, s32[4,6]{1,0:T(4,128)} %bitcast.18, f32[512,256]{1,0:T(8,128)} %rhs_ref.1, f32[2048,512]{1,0:T(8,128)} %linv_hbm.1, f32[6,1024,512]{2,1,0:T(8,128)} %bitcast.14, f32[64,1024]{1,0:T(8,128)} %bitcast.16, ...), custom_call_target="tpu_custom_call" | custom-call | flops 7000000000 | bytes 44000000 | tf_op jit(solution)/shard_map/pallas_call | solution.py:700
  148.3 2.0 %shard_map.104 = (f32[512,256]{1,0:T(8,128)}, f32[64,1024]{1,0:T(8,128)}, f32[64]{0:T(128)}) custom-call(f32[512,256]{1,0:T(8,128)} %get-tuple-element.9.y_in, f32[64,1024]{1,0:T(8,128)} %get-tuple-element.10.s_in, f32[8,128]{1,0:T(8,128)} %get-tuple-element.11.w_in), custom_call_target="tpu_custom_call" | custom-call | tf_op jit(solution)/shard_map/pallas_call | solution.py:740

commit v6 on v5

--- a/solution.py
+++ b/solution.py
@@ -52,9 +52,9 @@
 def kernel(order_ref, mask_ref, rhs_ref, linv_hbm, lpan_hbm, srhs_hbm, sinv_hbm, span_hbm,
            leafy_hbm, sol_hbm, width_ref,
            abuf, xbuf, xh, xl, lbuf, zs, zr, za, ybuf, yh_s, yl_s, pbuf, own, snd, rcv, zrs,
-           pk1, pk, zpair, yrs, s2, grecv, ubuf, accp, pend, squares, cacc, racc, rhsv, rhsp, vcat, vh0, solv, invb, spb, csend, crecv, relay, xrs, qsend, qrecv, top, wsend, wrecv,
+           pk1, pk, zpair, yrs, s2, grecv, ubuf, accp, pend, squares, cacc, racc, rhsv, rhsp, vcat, vh0, solv, invb, spb, csend, crecv, third, xrs, qsend, qrecv, top, wsend, wrecv,
            ld_sem, lp_sem, sp_sem, a2a_sem, zs_sem, zr_sem, za_sem, us_sem, ur_sem, rs_sem, rr_sem,
-           relay_sem, xr_sem, q_sem, qr_sem, top_sem, ps_sem, p3_sem, pair_sem, ys_sem, yr_sem, g_sem, u_sem, cs_sem, cr_sem, w_sem, out_sem):
+           third_sem, xr_sem, q_sem, qr_sem, top_sem, ps_sem, p3_sem, pair_sem, ys_sem, yr_sem, g_sem, u_sem, cs_sem, cr_sem, w_sem, out_sem):
     leaf = lax.axis_index("leaf")
     grid = lax.axis_index("grid")
     me = leaf * 4 + grid
@@ -376,48 +376,54 @@
             src_ref=csend.at[1, pl.ds(0, 512)], dst_ref=grecv.at[place],
             send_sem=cs_sem.at[1, 0], recv_sem=g_sem.at[place], device_id=(above, grid), device_id_type=MESH)
 
-    def relay_copy():
-        return pltpu.make_async_remote_copy(
-            src_ref=csend.at[2, pl.ds(0, 512)], dst_ref=relay.at[side],
-            send_sem=cs_sem.at[2, 0], recv_sem=relay_sem.at[side], device_id=(parent, grid), device_id_type=MESH)
-
-    def x_copy(m, u, k):
-        q = lax.rem(x + k, 4)
+    def ring_copy(m, u, k):
+        over_z = u < 2
+        q = lax.rem(jnp.where(over_z, z, x) + k, 4)
         return pltpu.make_async_remote_copy(
             src_ref=csend.at[m, rows(q * 128, 128)], dst_ref=xrs.at[u, 3 - k],
             send_sem=cs_sem.at[m, k], recv_sem=xr_sem.at[u, 3 - k],
-            device_id=((q * 4 + z) * 2 + yl, grid), device_id_type=MESH)
+            device_id=((jnp.where(over_z, x, q) * 4 + jnp.where(over_z, q, z)) * 2 + yl, grid), device_id_type=MESH)
+
+    def side_copy(u):
+        return pltpu.make_async_remote_copy(
+            src_ref=qsend.at[u], dst_ref=third.at[u, rows(z * 128, 128)],
+            send_sem=q_sem.at[u], recv_sem=third_sem.at[u], device_id=(leaf_3, grid), device_id_type=MESH)
 
     def quarter_copy(u):
         return pltpu.make_async_remote_copy(
-            src_ref=qsend.at[u], dst_ref=qrecv.at[u, side],
-            send_sem=q_sem.at[u], recv_sem=qr_sem.at[u, side], device_id=(parent, grid), device_id_type=MESH)
+            src_ref=qsend.at[u], dst_ref=qrecv.at[u - 2, side],
+            send_sem=q_sem.at[u], recv_sem=qr_sem.at[u - 2, side], device_id=(parent, grid), device_id_type=MESH)
 
     def top_copy(u):
         return pltpu.make_async_remote_copy(
             src_ref=qsend.at[u], dst_ref=top.at[rows(x * 128, 128)],
-            send_sem=q_sem.at[u], recv_sem=top_sem, device_id=(15 + 16 * u, grid), device_id_type=MESH)
-
-    def x_sum(u):
+            send_sem=q_sem.at[u], recv_sem=top_sem, device_id=(16 * u - 17, grid), device_id_type=MESH)
+
+    def ring_sum(u):
         for k in range(3):
             pltpu.make_async_copy(xrs.at[u, k], xrs.at[u, k], xr_sem.at[u, k]).wait()
-        m = 4 - level + u
-        qsend[u] = csend[m, rows(x * 128, 128), :] + xrs[u, 0] + (xrs[u, 1] + xrs[u, 2])
+        m = 2 - level + u
+        base = jnp.where(u < 2, z, x) * 128
+        qsend[u] = csend[m, rows(base, 128), :] + xrs[u, 0] + (xrs[u, 1] + xrs[u, 2])
+
+        @pl.when(u < 2)
+        def _():
+            side_copy(u).start()
 
         @pl.when(level > 1)
         def _():
             for s in range(2):
-                pltpu.make_async_copy(qrecv.at[u, s], qrecv.at[u, s], qr_sem.at[u, s]).wait()
-            qsend[u] = qsend[u] + (qrecv[u, 0] + qrecv[u, 1])
-
-        @pl.when(level < 3)
+                pltpu.make_async_copy(qrecv.at[u - 2, s], qrecv.at[u - 2, s], qr_sem.at[u - 2, s]).wait()
+            qsend[u] = qsend[u] + (qrecv[u - 2, 0] + qrecv[u - 2, 1])
+
+        @pl.when((u > 1) & (level < 3))
         def _():
             quarter_copy(u).start()
 
         @pl.when(level == 3)
         def _():
-            pltpu.make_async_copy(ubuf.at[pl.ds(0, 480)], ubuf.at[pl.ds(0, 480)], u_sem.at[2 + u]).wait()
-            start = (2 + u) * 512
+            pltpu.make_async_copy(ubuf.at[pl.ds(0, 480)], ubuf.at[pl.ds(0, 480)], u_sem.at[u]).wait()
+            start = u * 512
             value = qsend[u]
             for s in range(4):
                 value = value + ubuf[rows(start + s * 128, 128), :]
@@ -426,7 +432,8 @@
 
     def take_3(k, dst):
         pltpu.make_async_copy(ubuf.at[pl.ds(0, 480)], ubuf.at[pl.ds(0, 480)], u_sem.at[k]).wait()
-        dst[...] = ubuf[k * 512:(k + 1) * 512, :]
+        pltpu.make_async_copy(third.at[k], third.at[k], third_sem.at[k]).wait()
+        dst[...] = ubuf[k * 512:(k + 1) * 512, :] + third[k]
 
     def take_far(slot):
         pltpu.make_async_copy(grecv.at[slot], grecv.at[slot], g_sem.at[slot]).wait()
@@ -464,18 +471,17 @@
         @pl.when(level == 3)
         def _():
             take_3(0, accp)
-            take_3(1, pend)
 
         @pl.when(level > 3)
         def _():
             accp[...] = jnp.zeros_like(accp)
 
-        @pl.when((level > 2) & (level != 5))
+        @pl.when((level == 4) | (level == 6))
         def _():
             take_far(0)
             take_far(1)
 
-        @pl.when((level == 3) | (level == 4))
+        @pl.when(level == 4)
         def _():
             take_far(2)
             take_far(3)
@@ -524,6 +530,10 @@
                     squares[...] = squares[...] + jnp.sum(s_value * s_value, axis=0, keepdims=True)
                     squares[...] = squares[...] + crecv_squares()
                     csend[0, pl.ds(512, 8), :] = squares[...]
+
+                    @pl.when(level == 3)
+                    def _():
+                        take_3(1, pend)
                     for i in range(4):
                         out = pl.ds(i * 256, 256)
                         finished(cacc[out, :] + dot2(spb[0, out, k * 256:(k + 1) * 256], 1, part), 0, i)
@@ -558,26 +568,16 @@
         for i in range(4):
             out = pl.ds(i * 256, 256)
             finished(dot2(spb[slot, out, :], 1, slice(None)), m, i)
-        over_x = (level < 4) & (m >= 4 - level)
-
-        @pl.when((level == 2) & (m == 1))
-        def _():
-            for s in range(2):
-                pltpu.make_async_copy(relay.at[s], relay.at[s], relay_sem.at[s]).wait()
-            csend[1, pl.ds(0, 512), :] = csend[1, pl.ds(0, 512), :] + (relay[0] + relay[1])
-
-        @pl.when((m == 1) & jnp.logical_not(over_x))
+        far = (m == 1) & ((level == 2) | (level == 4))
+
+        @pl.when(far)
         def _():
             far_copy().start()
 
-        @pl.when((level == 1) & (m == 2))
-        def _():
-            relay_copy().start()
-
-        @pl.when(over_x)
+        @pl.when(jnp.logical_not(far))
         def _():
             for k in range(1, 4):
-                x_copy(m, m - 4 + level, k).start()
+                ring_copy(m, m + level - 2, k).start()
 
         @pl.when(m + 3 < n_pan)
         def _():
@@ -595,9 +595,9 @@
         def _():
             first_sum_2()
 
-        @pl.when((p > 0) & (p < 5))
-        def _():
-            first_sum(p + 1)
+        @pl.when(p < 4)
+        def _():
+            first_sum(p + 2)
 
         @pl.when(p == 1)
         def _():
@@ -617,9 +617,11 @@
         def _():
             panel(m)
 
-        @pl.when((level < 4) & ((m == 5 - level) | (m == 6 - level)))
-        def _():
-            x_sum(m - 5 + level)
+        u = m + level - 3
+
+        @pl.when((level < 4) & (u < 4) & ((u > 1) | ((level == 1) & (u >= 0))))
+        def _():
+            ring_sum(u)
         return carry
     lax.fori_loop(0, 8, phase, 0)
 
@@ -671,20 +673,16 @@
         for i in range(4):
             up_copy(i, 136 if i == 3 else 128).wait_send()
 
-    @pl.when((level < 3) | (level == 4))
+    @pl.when((level == 2) | (level == 4))
     def _():
         far_copy().wait_send()
 
-    @pl.when(level == 1)
-    def _():
-        relay_copy().wait_send()
-
-    @pl.when(level < 4)
-    def _():
-        for u in range(2):
-            for k in range(1, 4):
-                x_copy(4 - level + u, u, k).wait_send()
-            quarter_copy(u).wait_send()
+    def sent(u, carry):
+        for k in range(1, 4):
+            ring_copy(2 - level + u, u, k).wait_send()
+        pltpu.make_async_copy(qsend.at[u], qsend.at[u], q_sem.at[u]).wait()
+        return carry
+    lax.fori_loop(jnp.where(level == 1, 0, jnp.where(level < 4, 2, 4)), 4, sent, 0)
 
 
 def write_out(y_in, s_in, w_in, y_out, s_out, w_out):
@@ -726,11 +724,11 @@
             V((64, 1024), F32),
             V((1024, 1024), F32), V((3, 1024, 1024), F32),
             V((5, 520, 128), F32), V((2, 520, 128), F32), V((2, 512, 128), F32),
-            V((2, 3, 128, 128), F32), V((2, 128, 128), F32), V((2, 2, 128, 128), F32), V((512, 128), F32),
+            V((4, 3, 128, 128), F32), V((4, 128, 128), F32), V((2, 2, 128, 128), F32), V((512, 128), F32),
             V((1, 8, 128), F32), V((1, 8, 128), F32),
             DMA((3,)), DMA((3,)), DMA((3,)), DMA((2,)), DMA((3,)), DMA((2,)), DMA, DMA((6,)), DMA((6,)),
             DMA((4, 3)), DMA((4, 3)),
-            DMA((2,)), DMA((2, 3)), DMA((2,)), DMA((2, 2)), DMA,
+            DMA((2,)), DMA((4, 3)), DMA((4,)), DMA((2, 2)), DMA,
             DMA((2,)), DMA((5, 2)), DMA((2,)), DMA((5, 3)), DMA((5, 3)), DMA((4,)), DMA((4,)), DMA((5, 4)), DMA((2, 4)), DMA((2,)), DMA((2,)),
         ],
         compiler_params=pltpu.CompilerParams(

time: 151 us -> 135 us (0.89)
  Pallas kernels: 150 us -> 133 us
    pallas_call x1, Pallas kernels: 148 us -> 131 us  [local(): pl.pallas_call(kernel, out_shape=(jax.ShapeDtypeStruct((512, 256), F32),...]
where the time goes in v6:
time: 135 us; the launch traced here: 133 us
  Pallas kernels  133 us (99%)
    pallas_call x1, Pallas kernels, local(): pl.pallas_call(kernel, out_shape=(jax.ShapeDtypeStruct((512, 256), F32),...  131 us

profile of v6, /device:TPU:16, one launch (start us, length us, event | category | flops | bytes accessed | tf_op | source)
XLA Modules:
  0.0 133.3 jit_solution(17453670280929264898)
XLA Ops:
  0.6 130.6 %shard_map.103 = (f32[512,256]{1,0:T(8,128)}, f32[64,1024]{1,0:T(8,128)}, f32[8,128]{1,0:T(8,128)}) custom-call(s32[4,128]{1,0:T(4,128)} %bitcast.17, s32[4,6]{1,0:T(4,128)} %bitcast.18, f32[512,256]{1,0:T(8,128)} %rhs_ref.1, f32[2048,512]{1,0:T(8,128)} %linv_hbm.1, f32[6,1024,512]{2,1,0:T(8,128)} %bitcast.14, f32[64,1024]{1,0:T(8,128)} %bitcast.16, ...), custom_call_target="tpu_custom_call" | custom-call | flops 7000000000 | bytes 44000000 | tf_op jit(solution)/shard_map/pallas_call | solution.py:698
  131.3 2.0 %shard_map.104 = (f32[512,256]{1,0:T(8,128)}, f32[64,1024]{1,0:T(8,128)}, f32[64]{0:T(128)}) custom-call(f32[512,256]{1,0:T(8,128)} %get-tuple-element.9.y_in, f32[64,1024]{1,0:T(8,128)} %get-tuple-element.10.s_in, f32[8,128]{1,0:T(8,128)} %get-tuple-element.11.w_in), custom_call_target="tpu_custom_call" | custom-call | tf_op jit(solution)/shard_map/pallas_call | solution.py:738

commit v7 on v6

--- a/solution.py
+++ b/solution.py
@@ -595,21 +595,22 @@
         def _():
             first_sum_2()
 
-        @pl.when(p < 4)
+        @pl.when((p > 0) & (p < 4))
         def _():
             first_sum(p + 2)
 
-        @pl.when(p == 1)
+        @pl.when((p > 1) & (p < 6))
+        def _():
+            second_sum(p, 32)
+
+        @pl.when(p == start_at)
+        def _():
+            head()
+
+        @pl.when(p == 0)
         def _():
             second_sum(1, 64)
-
-        @pl.when((p > 1) & (p < 6))
-        def _():
-            second_sum(p, 32)
-
-        @pl.when(p == start_at)
-        def _():
-            head()
+            first_sum(2)
 
         m = p - start_at
 

time: 135 us -> 137 us (1.015)
  Pallas kernels: 133 us -> 135 us
    pallas_call x1, Pallas kernels: 131 us -> 133 us  [local(): pl.pallas_call(kernel, out_shape=(jax.ShapeDtypeStruct((512, 256), F32),...]
where the time goes in v7:
time: 137 us; the launch traced here: 135 us
  Pallas kernels  135 us (99%)
    pallas_call x1, Pallas kernels, local(): pl.pallas_call(kernel, out_shape=(jax.ShapeDtypeStruct((512, 256), F32),...  133 us

profile of v7, /device:TPU:16, one launch (start us, length us, event | category | flops | bytes accessed | tf_op | source)
XLA Modules:
  0.0 135.2 jit_solution(8064231190961335952)
XLA Ops:
  0.6 132.6 %shard_map.103 = (f32[512,256]{1,0:T(8,128)}, f32[64,1024]{1,0:T(8,128)}, f32[8,128]{1,0:T(8,128)}) custom-call(s32[4,128]{1,0:T(4,128)} %bitcast.17, s32[4,6]{1,0:T(4,128)} %bitcast.18, f32[512,256]{1,0:T(8,128)} %rhs_ref.1, f32[2048,512]{1,0:T(8,128)} %linv_hbm.1, f32[6,1024,512]{2,1,0:T(8,128)} %bitcast.14, f32[64,1024]{1,0:T(8,128)} %bitcast.16, ...), custom_call_target="tpu_custom_call" | custom-call | flops 7000000000 | bytes 44000000 | tf_op jit(solution)/shard_map/pallas_call | solution.py:699
  133.2 2.0 %shard_map.104 = (f32[512,256]{1,0:T(8,128)}, f32[64,1024]{1,0:T(8,128)}, f32[64]{0:T(128)}) custom-call(f32[512,256]{1,0:T(8,128)} %get-tuple-element.9.y_in, f32[64,1024]{1,0:T(8,128)} %get-tuple-element.10.s_in, f32[8,128]{1,0:T(8,128)} %get-tuple-element.11.w_in), custom_call_target="tpu_custom_call" | custom-call | tf_op jit(solution)/shard_map/pallas_call | solution.py:739

commit v8 on v6

--- a/solution.py
+++ b/solution.py
@@ -52,9 +52,9 @@
 def kernel(order_ref, mask_ref, rhs_ref, linv_hbm, lpan_hbm, srhs_hbm, sinv_hbm, span_hbm,
            leafy_hbm, sol_hbm, width_ref,
            abuf, xbuf, xh, xl, lbuf, zs, zr, za, ybuf, yh_s, yl_s, pbuf, own, snd, rcv, zrs,
-           pk1, pk, zpair, yrs, s2, grecv, ubuf, accp, pend, squares, cacc, racc, rhsv, rhsp, vcat, vh0, solv, invb, spb, csend, crecv, third, xrs, qsend, qrecv, top, wsend, wrecv,
+           pk1, yr1, s1, pk, zpair, yrs, s2, grecv, ubuf, accp, pend, squares, cacc, racc, rhsv, rhsp, vcat, vh0, solv, invb, spb, csend, crecv, third, xrs, qsend, qrecv, top, wsend, wrecv,
            ld_sem, lp_sem, sp_sem, a2a_sem, zs_sem, zr_sem, za_sem, us_sem, ur_sem, rs_sem, rr_sem,
-           third_sem, xr_sem, q_sem, qr_sem, top_sem, ps_sem, p3_sem, pair_sem, ys_sem, yr_sem, g_sem, u_sem, cs_sem, cr_sem, w_sem, out_sem):
+           third_sem, xr_sem, q_sem, qr_sem, top_sem, ps_sem, y1_sem, p3_sem, pair_sem, ys_sem, yr_sem, g_sem, u_sem, cs_sem, cr_sem, w_sem, out_sem):
     leaf = lax.axis_index("leaf")
     grid = lax.axis_index("grid")
     me = leaf * 4 + grid
@@ -239,11 +239,17 @@
     leaf_2 = (x * 4 + z - lax.rem(z, 2)) * 2 + 1
     leaf_3 = x * 8 + 3
     half_z = lax.rem(z, 2)
-    piece_1 = (pk1, y * 520, 520, leaf_1, ps_sem)
+    piece_1 = (s1, y * 136, 136, leaf_1, ps_sem)
     piece_2 = (s2.at[0], half_z * 256 + y * 64, 64, leaf_2, p3_sem.at[0])
 
     def piece_3(t):
         return (s2.at[t - 1, :, pl.ds(0, 32)], (t - 2) * 512 + z * 128 + y * 32, 32, leaf_3, p3_sem.at[t - 1])
+
+    def first_copy(k):
+        q = lax.rem(y + k, 4)
+        return pltpu.make_async_remote_copy(
+            src_ref=pk1.at[:, q], dst_ref=yr1.at[3 - k], send_sem=y1_sem.at[0, k - 1], recv_sem=y1_sem.at[1, 3 - k],
+            device_id=((x * 4 + z) * 2 + lax.rem(q, 2), lax.div(q, 2) * 2 + c), device_id_type=MESH)
 
     def pair_copy():
         return pltpu.make_async_remote_copy(
@@ -275,14 +281,15 @@
                 top = own[t, rows(base, 128), :] + rcv[t, rows(base, 128), :]
                 bottom = own[t, rows(base + 128, 128), :] + rcv[t, rows(base + 128, 128), :]
                 p0, p1 = packed_pair(top, bottom)
-                pk1[0, rows(i * 128, 128), :] = p0
-                pk1[1, rows(i * 128, 128), :] = p1
+                pk1[0, i, pl.ds(0, 128), :] = p0
+                pk1[1, i, pl.ds(0, 128), :] = p1
+                pk1[0, i, pl.ds(128, 8), :] = squares_1
+                pk1[1, i, pl.ds(128, 8), :] = turned(squares_1)
                 return carry
+            squares_1 = own[0, pl.ds(1024, 8), :] + rcv[0, pl.ds(1024, 8), :]
             lax.fori_loop(0, 4, body, 0)
-            squares = own[0, pl.ds(1024, 8), :] + rcv[0, pl.ds(1024, 8), :]
-            pk1[0, pl.ds(512, 8), :] = squares
-            pk1[1, pl.ds(512, 8), :] = turned(squares)
-            send_pieces(*piece_1, u_sem.at[0])
+            for k in range(1, 4):
+                first_copy(k).start()
         else:
             def body(i, carry):
                 part = rows(i * 256, 256)
@@ -317,6 +324,11 @@
         if t > 0:
             spread(t - 1)
     spread(5)
+    for k in range(3):
+        pltpu.make_async_copy(yr1.at[k], yr1.at[k], y1_sem.at[1, k]).wait()
+    for part in range(2):
+        s1[part] = pk1[part, y] + yr1[0, part] + (yr1[1, part] + yr1[2, part])
+    send_pieces(*piece_1, u_sem.at[0])
 
     def ring_start(t, size):
         for k in range(1, 4):
@@ -459,9 +471,10 @@
 
         @pl.when(level == 1)
         def _():
-            pltpu.make_async_copy(ubuf.at[pl.ds(0, 1560)], ubuf.at[pl.ds(0, 1560)], u_sem.at[0]).wait()
-            accp[...] = ubuf[0:512, :] + ubuf[520:1032, :] + ubuf[1040:1552, :] + ubuf[1560:2072, :]
-            squares[...] = ubuf[512:520, :] + ubuf[1032:1040, :] + ubuf[1552:1560, :] + ubuf[2072:2080, :]
+            pltpu.make_async_copy(ubuf.at[pl.ds(0, 408)], ubuf.at[pl.ds(0, 408)], u_sem.at[0]).wait()
+            for q in range(4):
+                accp[q * 128:(q + 1) * 128, :] = ubuf[q * 136:q * 136 + 128, :]
+            squares[...] = ubuf[128:136, :]
 
         @pl.when(level == 2)
         def _():
@@ -657,6 +670,8 @@
     pltpu.make_async_copy(solv, sol_hbm, out_sem.at[1]).wait()
     for t in range(6):
         u_copy(t).wait_send()
+    for k in range(1, 4):
+        first_copy(k).wait_send()
     wait_pieces(*piece_1)
     pair_copy().wait_send()
     for k in range(1, 4):
@@ -713,7 +728,8 @@
             V((3, 1024, 512), F32),
             V((6, 1032, 128), F32), V((6, 1032, 128), F32), V((6, 1032, 128), F32),
             V((4, 3, 256, 128), F32),
-            V((2, 520, 128), F32), V((5, 2, 256, 128), F32),
+            V((2, 4, 136, 128), F32), V((3, 2, 136, 128), F32), V((2, 136, 128), F32),
+            V((5, 2, 256, 128), F32),
             V((512, 128), F32), V((5, 3, 2, 64, 128), F32),
             V((5, 2, 64, 128), F32), V((4, 512, 128), F32),
             V((2080, 128), F32),
@@ -729,7 +745,7 @@
             DMA((3,)), DMA((3,)), DMA((3,)), DMA((2,)), DMA((3,)), DMA((2,)), DMA, DMA((6,)), DMA((6,)),
             DMA((4, 3)), DMA((4, 3)),
             DMA((2,)), DMA((4, 3)), DMA((4,)), DMA((2, 2)), DMA,
-            DMA((2,)), DMA((5, 2)), DMA((2,)), DMA((5, 3)), DMA((5, 3)), DMA((4,)), DMA((4,)), DMA((5, 4)), DMA((2, 4)), DMA((2,)), DMA((2,)),
+            DMA((2,)), DMA((2, 3)), DMA((5, 2)), DMA((2,)), DMA((5, 3)), DMA((5, 3)), DMA((4,)), DMA((4,)), DMA((5, 4)), DMA((2, 4)), DMA((2,)), DMA((2,)),
         ],
         compiler_params=pltpu.CompilerParams(
             collective_id=0, has_side_effects=True, vmem_limit_bytes=62 * 2 ** 20),

time: 135 us -> 133 us (0.985); the launches traced: 133 us -> 133 us
  no operation moved by 1% of the time
where the time goes in v8:
time: 133 us
  Pallas kernels  132 us (99%)
    pallas_call x1, Pallas kernels, local(): pl.pallas_call(kernel, out_shape=(jax.ShapeDtypeStruct((512, 256), F32),...  130 us

profile of v8, /device:TPU:16, one launch (start us, length us, event | category | flops | bytes accessed | tf_op | source)
XLA Modules:
  0.0 132.9 jit_solution(14657116391364025637)
XLA Ops:
  0.6 130.2 %shard_map.103 = (f32[512,256]{1,0:T(8,128)}, f32[64,1024]{1,0:T(8,128)}, f32[8,128]{1,0:T(8,128)}) custom-call(s32[4,128]{1,0:T(4,128)} %bitcast.17, s32[4,6]{1,0:T(4,128)} %bitcast.18, f32[512,256]{1,0:T(8,128)} %rhs_ref.1, f32[2048,512]{1,0:T(8,128)} %linv_hbm.1, f32[6,1024,512]{2,1,0:T(8,128)} %bitcast.14, f32[64,1024]{1,0:T(8,128)} %bitcast.16, ...), custom_call_target="tpu_custom_call" | custom-call | flops 7000000000 | bytes 44000000 | tf_op jit(solution)/shard_map/pallas_call | solution.py:713
  130.9 2.0 %shard_map.104 = (f32[512,256]{1,0:T(8,128)}, f32[64,1024]{1,0:T(8,128)}, f32[64]{0:T(128)}) custom-call(f32[512,256]{1,0:T(8,128)} %get-tuple-element.9.y_in, f32[64,1024]{1,0:T(8,128)} %get-tuple-element.10.s_in, f32[8,128]{1,0:T(8,128)} %get-tuple-element.11.w_in), custom_call_target="tpu_custom_call" | custom-call | tf_op jit(solution)/shard_map/pallas_call | solution.py:754

commit v9 on v8

--- a/solution.py
+++ b/solution.py
@@ -302,7 +302,16 @@
                 for k in range(1, 4):
                     rs_copy(t, k).start()
 
+    def first_pieces():
+        for k in range(3):
+            pltpu.make_async_copy(yr1.at[k], yr1.at[k], y1_sem.at[1, k]).wait()
+        for part in range(2):
+            s1[part] = pk1[part, y] + yr1[0, part] + (yr1[1, part] + yr1[2, part])
+        send_pieces(*piece_1, u_sem.at[0])
+
     for t in range(6):
+        if t == 5:
+            first_pieces()
         lp_copy(t).wait()
         masks = [jnp.full((1, 256), mask_ref[b, t].astype(F32)).astype(BF16) for b in range(4)]
         masked = lambda ref: jnp.concatenate(
@@ -324,11 +333,6 @@
         if t > 0:
             spread(t - 1)
     spread(5)
-    for k in range(3):
-        pltpu.make_async_copy(yr1.at[k], yr1.at[k], y1_sem.at[1, k]).wait()
-    for part in range(2):
-        s1[part] = pk1[part, y] + yr1[0, part] + (yr1[1, part] + yr1[2, part])
-    send_pieces(*piece_1, u_sem.at[0])
 
     def ring_start(t, size):
         for k in range(1, 4):

time: 133 us -> 134 us (level)
  Pallas kernels: 132 us -> 134 us
where the time goes in v9:
time: 134 us
  Pallas kernels  134 us (100%)
    pallas_call x1, Pallas kernels, local(): pl.pallas_call(kernel, out_shape=(jax.ShapeDtypeStruct((512, 256), F32),...  132 us

profile of v9, /device:TPU:16, one launch (start us, length us, event | category | flops | bytes accessed | tf_op | source)
XLA Modules:
  0.0 134.2 jit_solution(11186619545210153746)
XLA Ops:
  0.6 131.5 %shard_map.103 = (f32[512,256]{1,0:T(8,128)}, f32[64,1024]{1,0:T(8,128)}, f32[8,128]{1,0:T(8,128)}) custom-call(s32[4,128]{1,0:T(4,128)} %bitcast.17, s32[4,6]{1,0:T(4,128)} %bitcast.18, f32[512,256]{1,0:T(8,128)} %rhs_ref.1, f32[2048,512]{1,0:T(8,128)} %linv_hbm.1, f32[6,1024,512]{2,1,0:T(8,128)} %bitcast.14, f32[64,1024]{1,0:T(8,128)} %bitcast.16, ...), custom_call_target="tpu_custom_call" | custom-call | flops 7000000000 | bytes 44000000 | tf_op jit(solution)/shard_map/pallas_call | solution.py:717
  132.1 2.0 %shard_map.104 = (f32[512,256]{1,0:T(8,128)}, f32[64,1024]{1,0:T(8,128)}, f32[64]{0:T(128)}) custom-call(f32[512,256]{1,0:T(8,128)} %get-tuple-element.9.y_in, f32[64,1024]{1,0:T(8,128)} %get-tuple-element.10.s_in, f32[8,128]{1,0:T(8,128)} %get-tuple-element.11.w_in), custom_call_target="tpu_custom_call" | custom-call | tf_op jit(solution)/shard_map/pallas_call | solution.py:758

commit v10 on v8

--- a/solution.py
+++ b/solution.py
@@ -52,9 +52,9 @@
 def kernel(order_ref, mask_ref, rhs_ref, linv_hbm, lpan_hbm, srhs_hbm, sinv_hbm, span_hbm,
            leafy_hbm, sol_hbm, width_ref,
            abuf, xbuf, xh, xl, lbuf, zs, zr, za, ybuf, yh_s, yl_s, pbuf, own, snd, rcv, zrs,
-           pk1, yr1, s1, pk, zpair, yrs, s2, grecv, ubuf, accp, pend, squares, cacc, racc, rhsv, rhsp, vcat, vh0, solv, invb, spb, csend, crecv, third, xrs, qsend, qrecv, top, wsend, wrecv,
+           pk1, yr1, s1, pk, zpair, yrs, s2, grecv, ubuf, accp, pend, squares, cacc, racc, rhsv, rhsp, vcat, vh0, solv, invb, spb, csend, crecv, third, peer, xrs, qsend, qrecv, top, wsend, wrecv,
            ld_sem, lp_sem, sp_sem, a2a_sem, zs_sem, zr_sem, za_sem, us_sem, ur_sem, rs_sem, rr_sem,
-           third_sem, xr_sem, q_sem, qr_sem, top_sem, ps_sem, y1_sem, p3_sem, pair_sem, ys_sem, yr_sem, g_sem, u_sem, cs_sem, cr_sem, w_sem, out_sem):
+           third_sem, peer_sem, xr_sem, q_sem, qr_sem, top_sem, ps_sem, y1_sem, p3_sem, pair_sem, ys_sem, yr_sem, g_sem, u_sem, cs_sem, cr_sem, w_sem, out_sem):
     leaf = lax.axis_index("leaf")
     grid = lax.axis_index("grid")
     me = leaf * 4 + grid
@@ -379,6 +379,12 @@
             src_ref=csend.at[0, part], dst_ref=crecv.at[side, part],
             send_sem=cs_sem.at[0, i], recv_sem=cr_sem.at[side, i], device_id=(parent, grid), device_id_type=MESH)
 
+    def peer_copy(i, size):
+        part = rows(i * 128, size)
+        return pltpu.make_async_remote_copy(
+            src_ref=csend.at[0, part], dst_ref=peer.at[part],
+            send_sem=cs_sem.at[0, i], recv_sem=peer_sem.at[i], device_id=(jnp.maximum(leaf - 8, 0), grid), device_id_type=MESH)
+
     def wait_child(s, i, size):
         part = rows(i * 128, size)
         pltpu.make_async_copy(csend.at[0, part], crecv.at[s, part], cr_sem.at[s, i]).wait()
@@ -517,7 +523,7 @@
                 wait_child(0, k, size)
                 accp[packed, :] = accp[packed, :] + crecv[0, packed, :]
 
-            @pl.when((level > 1) & (level < 6))
+            @pl.when((level > 1) & (level < 6) & (level != 4))
             def _():
                 wait_child(1, k, size)
                 accp[packed, :] = accp[packed, :] + crecv[1, packed, :]
@@ -555,7 +561,22 @@
                         def _():
                             up = pl.ds(i * 128, 128)
                             csend[0, up, :] = csend[0, up, :] + pend[up, :]
-                        up_copy(i, 136 if i == 3 else 128).start()
+                        size = 136 if i == 3 else 128
+
+                        @pl.when(level != 3)
+                        def _():
+                            up_copy(i, size).start()
+
+                        @pl.when((level == 3) & (lax.rem(x, 2) == 1))
+                        def _():
+                            peer_copy(i, size).start()
+
+                        @pl.when((level == 3) & (lax.rem(x, 2) == 0))
+                        def _():
+                            peer_copy(i, size).wait_recv()
+                            both = pl.ds(i * 128, size)
+                            csend[0, both, :] = csend[0, both, :] + peer[both, :]
+                            up_copy(i, size).start()
             solv[:, k * 256:(k + 1) * 256] = jnp.transpose(s_value)[:64]
             if k < 3:
                 squares[...] = squares[...] + jnp.sum(s_value * s_value, axis=0, keepdims=True)
@@ -573,7 +594,8 @@
         pltpu.make_async_copy(solv, sol_hbm, out_sem.at[1]).start()
 
     def crecv_squares():
-        return jnp.where(level > 1, crecv[0, pl.ds(512, 8), :] + crecv[1, pl.ds(512, 8), :], 0.0)
+        second = jnp.where(level == 4, 0.0, crecv[1, pl.ds(512, 8), :])
+        return jnp.where(level > 1, crecv[0, pl.ds(512, 8), :] + second, 0.0)
 
     def panel(m):
         sp_copy(m).wait()
@@ -739,12 +761,12 @@
             V((2, 1024, 128), BF16), V((2, 1024, 128), BF16),
             V((64, 1024), F32),
             V((1024, 1024), F32), V((3, 1024, 1024), F32),
-            V((5, 520, 128), F32), V((2, 520, 128), F32), V((2, 512, 128), F32),
+            V((5, 520, 128), F32), V((2, 520, 128), F32), V((2, 512, 128), F32), V((520, 128), F32),
             V((4, 3, 128, 128), F32), V((4, 128, 128), F32), V((2, 2, 128, 128), F32), V((512, 128), F32),
             V((1, 8, 128), F32), V((1, 8, 128), F32),
             DMA((3,)), DMA((3,)), DMA((3,)), DMA((2,)), DMA((3,)), DMA((2,)), DMA, DMA((6,)), DMA((6,)),
             DMA((4, 3)), DMA((4, 3)),
-            DMA((2,)), DMA((4, 3)), DMA((4,)), DMA((2, 2)), DMA,
+            DMA((2,)), DMA((4,)), DMA((4, 3)), DMA((4,)), DMA((2, 2)), DMA,
             DMA((2,)), DMA((2, 3)), DMA((5, 2)), DMA((2,)), DMA((5, 3)), DMA((5, 3)), DMA((4,)), DMA((4,)), DMA((5, 4)), DMA((2, 4)), DMA((2,)), DMA((2,)),
         ],
         compiler_params=pltpu.CompilerParams(

time: 133 us -> 136 us (1.023); the launches traced: 133 us -> 134 us
  Pallas kernels: 132 us -> 134 us
where the time goes in v10:
time: 136 us; the launch traced here: 134 us
  Pallas kernels  134 us (99%)
    pallas_call x1, Pallas kernels, local(): pl.pallas_call(kernel, out_shape=(jax.ShapeDtypeStruct((512, 256), F32),...  131 us

profile of v10, /device:TPU:16, one launch (start us, length us, event | category | flops | bytes accessed | tf_op | source)
XLA Modules:
  0.0 134.2 jit_solution(8164293358106516806)
XLA Ops:
  0.6 131.5 %shard_map.103 = (f32[512,256]{1,0:T(8,128)}, f32[64,1024]{1,0:T(8,128)}, f32[8,128]{1,0:T(8,128)}) custom-call(s32[4,128]{1,0:T(4,128)} %bitcast.17, s32[4,6]{1,0:T(4,128)} %bitcast.18, f32[512,256]{1,0:T(8,128)} %rhs_ref.1, f32[2048,512]{1,0:T(8,128)} %linv_hbm.1, f32[6,1024,512]{2,1,0:T(8,128)} %bitcast.14, f32[64,1024]{1,0:T(8,128)} %bitcast.16, ...), custom_call_target="tpu_custom_call" | custom-call | flops 7000000000 | bytes 44000000 | tf_op jit(solution)/shard_map/pallas_call | solution.py:735
  132.1 2.0 %shard_map.104 = (f32[512,256]{1,0:T(8,128)}, f32[64,1024]{1,0:T(8,128)}, f32[64]{0:T(128)}) custom-call(f32[512,256]{1,0:T(8,128)} %get-tuple-element.9.y_in, f32[64,1024]{1,0:T(8,128)} %get-tuple-element.10.s_in, f32[8,128]{1,0:T(8,128)} %get-tuple-element.11.w_in), custom_call_target="tpu_custom_call" | custom-call | tf_op jit(solution)/shard_map/pallas_call | solution.py:776
